TPU v7x, 512 devices: a whole 4x8x8 slice. The times are simulated.
512 devices in a mesh: ka: 8 (over z), pb: 64 (over y, x, core).
Axes of the slice: x: 4, y: 8, z: 8, core: 2. Of those that a mesh axis runs over, the one named last changes fastest.
Arguments:
- wannier_g: bfloat16 [8, 1920, 13824], P('ka', 'pb'), may hold values from -0.125 to 0.125
- rotations: float32 [512, 512], P(('ka', 'pb')), may hold values from -1 to 1
- home_rows: int32 [512], replicated, may hold values from 0 to 511, each once
- shifted: int32 [8, 512], P('ka', 'pb'), may hold values from 0 to 511, as said below
- band_count: int32 [8, 512], P('ka', 'pb'), may hold values from 4 to 16
- lattice: int32 [3, 1920], replicated, may hold values from -6 to 6
Outputs:
- bloch_g: bfloat16 [8, 512, 13824], P('ka', 'pb')
Inputs may be any that keep to these rules, and one draw needn't show every extreme that they name: shifted[q, k] is the fine point whose grid coordinates are those of k plus those of one fine point drawn for q, modulo 8. `home_rows`: each fine point is held by exactly one row.
All inputs are finite; a program needn't handle non-finite values.
Results may differ from a plain program's by a relative error of at most 0.0049.
Values may be sent and summed in bfloat16 or wider, within the bound.
A program may use at most 64 MiB of HBM per device.

v0:
```python
import jax
import jax.numpy as jnp
from jax import lax
from jax.sharding import PartitionSpec as P

NW = 16
NMODE = 27
NKG = 8
K = 512


def phase_table(lattice):
    points = jnp.arange(K, dtype=jnp.int32)
    first_coord = points // (NKG * NKG)
    second_coord = points // NKG % NKG
    third_coord = points % NKG
    winding = (
        first_coord[:, None] * lattice[0][None, :]
        + second_coord[:, None] * lattice[1][None, :]
        + third_coord[:, None] * lattice[2][None, :]
    )
    winding = jnp.mod(winding, NKG)
    angles = winding.astype(jnp.float32) * (2.0 * jnp.pi / NKG)
    return jnp.concatenate([jnp.cos(angles), jnp.sin(angles)], axis=0).astype(jnp.bfloat16)


def combine(summed):
    leading = summed.shape[:-2]
    points = summed.shape[-2] // 2
    width = summed.shape[-1]
    halves = summed.reshape(leading + (2, points, width // 2, 2))
    cosine = halves[..., 0, :, :, :]
    sine_part = halves[..., 1, :, :, :]
    real_out = cosine[..., 0] - sine_part[..., 1]
    imag_out = sine_part[..., 0] + cosine[..., 1]
    return (
        jnp.stack([real_out, imag_out], axis=-1)
        .reshape(leading + (points, width))
        .astype(jnp.bfloat16)
    )


def lattice_sum(segment, phases):
    summed = jnp.einsum("kr,qrc->qkc", phases, segment, preferred_element_type=jnp.float32)
    return combine(summed)


def rotate(tiles, rot_right, rot_left, counts):

    def contract(form, first_op, second_op):
        return jnp.einsum(form, first_op, second_op, precision=lax.Precision.HIGHEST)

    real_tile, imag_tile = (tiles[..., 0], tiles[..., 1])
    real_right, imag_right = (rot_right[..., 0], rot_right[..., 1])
    real_left, imag_left = (rot_left[..., 0], rot_left[..., 1])
    first_form = "...mnv,...nj->...mjv"
    real_mid = contract(first_form, real_tile, real_right) - contract(
        first_form, imag_tile, imag_right
    )
    imag_mid = contract(first_form, real_tile, imag_right) + contract(
        first_form, imag_tile, real_right
    )
    second_form = "...mi,...mjv->...ijv"
    real_out = contract(second_form, real_left, real_mid) + contract(
        second_form, imag_left, imag_mid
    )
    imag_out = contract(second_form, real_left, imag_mid) - contract(
        second_form, imag_left, real_mid
    )
    band_index = jnp.arange(NW, dtype=jnp.int32)
    limit = counts[..., None, None]
    inside = (band_index[:, None] < limit) & (band_index[None, :] < limit)
    inside = inside[..., None]
    zeros = jnp.zeros_like(real_out)
    return jnp.stack(
        [jnp.where(inside, real_out, zeros), jnp.where(inside, imag_out, zeros)], axis=-1
    )


def per_device(wannier_g, rotations, home_rows, shifted, band_count, lattice):
    phases = phase_table(lattice)
    columns = lax.all_to_all(wannier_g, "pb", split_axis=2, concat_axis=1, tiled=True)
    bloch_tiles = lax.all_to_all(
        lattice_sum(columns, phases), "pb", split_axis=1, concat_axis=2, tiled=True
    )
    q_dev, k_dev = shifted.shape
    offset = lax.axis_index("pb") * k_dev
    own_points = offset + jnp.arange(k_dev, dtype=jnp.int32)
    wanted = jnp.concatenate([own_points, shifted.reshape(-1)])
    picker = (home_rows[None, :] == wanted[:, None]).astype(jnp.float32)
    gathered = lax.all_gather(rotations, ("ka", "pb"), axis=0, tiled=True)
    picked = jnp.dot(
        picker, gathered, precision=lax.Precision.HIGHEST, preferred_element_type=jnp.float32
    )
    rot_right = picked[:k_dev].reshape(1, k_dev, NW, NW, 2)
    rot_left = picked[k_dev:].reshape(q_dev, k_dev, NW, NW, 2)
    tile_float = bloch_tiles.astype(jnp.float32).reshape(q_dev, k_dev, NW, NW, NMODE, 2)
    rotated = rotate(tile_float, rot_right, rot_left, band_count)
    return rotated.reshape(q_dev, k_dev, NW * NW * NMODE * 2).astype(jnp.bfloat16)


def solution(mesh):
    placed = (P("ka", "pb", None), P(("ka", "pb"), None), P(), P("ka", "pb"), P("ka", "pb"), P())
    return jax.shard_map(
        per_device, mesh=mesh, in_specs=placed, out_specs=P("ka", "pb", None), check_vma=False
    )
```

profile of v0, /device:TPU:1, one launch (start us, length us, event | category | flops | bytes accessed | tf_op | source)
XLA Modules:
  0.0 264.0 jit_solution(17335581533455124109)
XLA Ops:
  6.5 13.8 %copy.77 = bf16[1,30,13824]{1,0,2:T(2,128)(2,1)} copy(bf16[1,30,13824]{2,1,0:T(8,128)(2,1)} %param.6) | data formatting | bytes 1658880 | tf_op args[0]
  20.3 0.5 broadcast.168
  20.9 75.3 %reduce.6 = bf16[13824,30]{1,0:T(8,128)(2,1)S(1)} reduce(bf16[13824,1,30]{2,1,0:T(2,128)(2,1)} %bitcast.100, bf16[]{:T(256)} %broadcast.168), dimensions={1}, to_apply=%bitcast.91.reduce_sub_computation | reduce | bytes 1658882
  96.2 0.0 copy-start.3
  96.2 5.3 %reshape.246 = bf16[64,2,3240]{2,1,0:T(2,128)(2,1)} reshape(bf16[13824,30]{1,0:T(8,128)(2,1)S(1)} %reduce.6) | data formatting | bytes 1658880
  101.5 11.6 %all-to-all-start = ((bf16[64,2,3240]{2,1,0:T(2,128)(2,1)}), bf16[64,2,3240]{2,1,0:T(2,128)(2,1)S(1)}, u32[]{:S(2)}, u32[]{:S(2)}) async-start(bf16[64,2,3240]{2,1,0:T(2,128)(2,1)} %reshape.246), calls=%async_computation | async-start | bytes 1703936 | tf_op jit(solution)/shard_map/all_to_all | solution.py:82
  113.1 0.2 all-gather.3.cloned.1.call-start
  113.4 0.5 all-gather.3.cloned.1.call-update
  113.9 0.0 copy-done.3
  113.9 0.7 pad_add_fusion
  114.6 0.9 slice_reduce_fusion.2
  115.5 17.8 %cosine_convert_fusion = (bf16[512,1920]{1,0:T(8,128)(2,1)}, bf16[512,1920]{1,0:T(8,128)(2,1)}) fusion(s32[1920]{0:T(1024)S(1)} %get-tuple-element.6, s32[512]{0:T(512)S(1)} %get-tuple-element.22, s32[1920]{0:T(1024)S(1)} %get-tuple-element.7, s32[512]{0:T(512)S(1)} %get-tuple-element.23, s32[1920]{0:T(1024)S(1)} %get-tuple-element.5, ...), kind=kLoop, calls=%fused_computation.11 | loop fusion | flops 19660800 | bytes 3961344 | tf_op jit(solution)/shard_map/convert.6
  133.3 3.8 %all-to-all-done = bf16[64,2,3240]{2,1,0:T(2,128)(2,1)S(1)} async-done(((bf16[64,2,3240]{2,1,0:T(2,128)(2,1)}), bf16[64,2,3240]{2,1,0:T(2,128)(2,1)S(1)}, u32[]{:S(2)}, u32[]{:S(2)}) %all-to-all-start) | async-done | bytes 829472 | tf_op jit(solution)/shard_map/all_to_all | solution.py:82
  137.1 9.1 %reshape.247 = bf16[13824,1,30]{2,1,0:T(2,128)(2,1)} reshape(bf16[64,2,3240]{2,1,0:T(2,128)(2,1)S(1)} %all-to-all-done) | data formatting | bytes 1658880
  146.2 13.3 %copy.78 = bf16[1,30,13824]{2,1,0:T(8,128)(2,1)S(1)} copy(bf16[1,30,13824]{1,0,2:T(2,128)(2,1)} %bitcast.101) | data formatting | bytes 1658880 | tf_op jit(solution)/shard_map/all_to_all | solution.py:82
  159.4 3.1 %all_to_all.23 = bf16[1,30,64,216]{3,2,1,0:T(8,128)(2,1)S(1)} reshape(bf16[1,30,13824]{2,1,0:T(8,128)(2,1)S(1)} %copy.78) | data formatting | bytes 1658880 | tf_op jit(solution)/shard_map/all_to_all | solution.py:82
  162.5 0.6 copy.79
  163.1 0.5 reshape.228
  163.5 3.6 %fusion.11 = f32[1,1024,216]{1,2,0:T(8,128)S(1)} fusion(bf16[1920,216]{1,0:T(8,128)(2,1)S(1)} %reshape.228, bf16[512,1920]{1,0:T(8,128)(2,1)} %get-tuple-element.21, bf16[512,1920]{1,0:T(8,128)(2,1)} %get-tuple-element.20), kind=kOutput, calls=%fused_computation.20 | convolution fusion | flops 857210880 | bytes 5646336 | tf_op jit(solution)/shard_map/kr,qrc->qkc/dot_general | solution.py:44
  167.1 0.7 reshape.229
  167.9 0.0 copy-start.4
  167.9 0.7 fusion.55
  168.6 0.2 copy.123
  168.8 0.2 copy.124
  169.1 0.5 fusion.34
  169.6 0.5 pad_maximum_fusion.1
  170.1 0.1 convert_element_type.31
  170.2 0.6 copy.82
  170.8 2.3 reduce.7
  173.1 1.2 reshape.248
  174.3 6.5 %all-to-all-start.1 = ((bf16[64,2,864]{2,1,0:T(2,128)(2,1)}), bf16[64,2,864]{2,1,0:T(2,128)(2,1)S(1)}, u32[]{:S(2)}, u32[]{:S(2)}) async-start(bf16[64,2,864]{2,1,0:T(2,128)(2,1)} %reshape.248), calls=%async_computation.1 | async-start | bytes 458752 | tf_op jit(solution)/shard_map/all_to_all | solution.py:83
  180.9 0.0 copy-done.4
  180.9 0.1 iota_compare_fusion
  180.9 0.1 broadcast_and_fusion
  181.0 12.3 %all-to-all-done.1 = bf16[64,2,864]{2,1,0:T(2,128)(2,1)S(1)} async-done(((bf16[64,2,864]{2,1,0:T(2,128)(2,1)}), bf16[64,2,864]{2,1,0:T(2,128)(2,1)S(1)}, u32[]{:S(2)}, u32[]{:S(2)}) %all-to-all-start.1) | async-done | bytes 221216 | tf_op jit(solution)/shard_map/all_to_all | solution.py:83
  193.4 0.5 reshape.249
  193.9 0.7 copy.125
  194.7 3.3 %copy.83 = bf16[1,8,64,216]{1,3,2,0:T(8,128)(2,1)S(1)} copy(bf16[1,8,64,216]{3,1,2,0:T(8,128)(2,1)} %bitcast.110) | data formatting | bytes 442368 | tf_op jit(solution)/shard_map/all_to_all | solution.py:83
  198.0 8.7 %fusion.54 = (bf16[1,8,16,16,27,1]{1,5,4,3,2,0:T(2,128)(2,1)}, bf16[1,8,16,16,27,1]{1,5,4,3,2,0:T(2,128)(2,1)}) fusion(bf16[1,8,16,16,27,2]{1,5,4,3,2,0:T(2,128)(2,1)S(1)} %bitcast.99), kind=kLoop, calls=%fused_computation.86 | loop fusion | bytes 442368 | tf_op jit(solution)/shard_map/slice | solution.py:53
  206.7 8.8 %copy.104 = bf16[1,8,16,16,27,1]{4,3,2,1,5,0:T(8,128)(2,1)} copy(bf16[1,8,16,16,27,1]{1,5,4,3,2,0:T(2,128)(2,1)} %get-tuple-element.9) | data formatting | bytes 221184
  215.4 5.7 %copy.106 = bf16[1,8,16,16,27,1]{4,3,2,1,5,0:T(8,128)(2,1)} copy(bf16[1,8,16,16,27,1]{1,5,4,3,2,0:T(2,128)(2,1)S(1)} %copy-done) | data formatting | bytes 221184
  221.1 12.8 %all-gather.3.cloned.1.call-done = f32[512,1,512]{2,1,0:T(1,128)} async-done(((f32[1,1,512]{2,1,0:T(1,128)}), f32[512,1,512]{2,1,0:T(1,128)}) %all-gather.3.cloned.1.call-update) | async-done | bytes 1048592 | tf_op jit(solution)/shard_map/all_gather | solution.py:91
  233.9 1.7 fusion.18
  235.6 0.1 copy.75
  235.8 0.2 fusion.57
  236.0 0.1 copy.105
  236.1 0.1 copy.103
  236.2 0.1 copy.73
  236.4 0.2 fusion.56
  236.6 0.1 copy.102
  236.7 1.6 fusion.29
  238.3 0.0 copy-done.1
  238.3 0.6 fusion.31
  238.9 0.0 copy-done.2
  238.9 0.6 fusion.9
  239.4 0.6 fusion.10
  240.0 0.1 copy.107
  240.1 1.2 fusion.21
  241.4 1.2 fusion.25
  242.6 1.3 fusion.17
  243.9 1.3 fusion.16
  245.2 1.2 pad_maximum_fusion
  246.4 8.6 %copy.92 = bf16[1,8,16,16,27,2]{1,5,4,3,2,0:T(2,128)(2,1)S(1)} copy(bf16[1,8,16,16,27,2]{4,2,3,1,5,0:T(8,128)(2,1)} %pad_maximum_fusion) | data formatting | bytes 442368 | tf_op jit(solution)/shard_map/stack | solution.py:75
  255.0 2.1 copy.93
  (8 shorter events, 0.0 us)
Async XLA Ops:
  96.2 17.7 %copy-start.3 = (s32[1,8]{1,0:T(1,128)S(1)}, s32[1,8]{1,0:T(1,128)}, u32[]{:S(2)}) copy-start(s32[1,8]{1,0:T(1,128)} %param.9) | copy-start | bytes 100
  101.5 35.6 %all-to-all-start = ((bf16[64,2,3240]{2,1,0:T(2,128)(2,1)}), bf16[64,2,3240]{2,1,0:T(2,128)(2,1)S(1)}, u32[]{:S(2)}, u32[]{:S(2)}) async-start(bf16[64,2,3240]{2,1,0:T(2,128)(2,1)} %reshape.246), calls=%async_computation | async-start | bytes 1703936 | tf_op jit(solution)/shard_map/all_to_all | solution.py:82
  113.1 120.8 %all-gather.3.cloned.1.call-start = ((), (), s32[]{:S(2)}) async-start(), calls=%async_computation.2 | async-start | bytes 1050624 | tf_op jit(solution)/shard_map/all_gather | solution.py:91
  167.9 13.0 %copy-start.4 = (s32[1,8]{1,0:T(1,128)S(1)}, s32[1,8]{1,0:T(1,128)}, u32[]{:S(2)}) copy-start(s32[1,8]{1,0:T(1,128)} %param.10) | copy-start | bytes 100
  174.3 19.0 %all-to-all-start.1 = ((bf16[64,2,864]{2,1,0:T(2,128)(2,1)}), bf16[64,2,864]{2,1,0:T(2,128)(2,1)S(1)}, u32[]{:S(2)}, u32[]{:S(2)}) async-start(bf16[64,2,864]{2,1,0:T(2,128)(2,1)} %reshape.248), calls=%async_computation.1 | async-start | bytes 458752 | tf_op jit(solution)/shard_map/all_to_all | solution.py:83
  206.7 8.8 %copy-start = (bf16[1,8,16,16,27,1]{1,5,4,3,2,0:T(2,128)(2,1)S(1)}, bf16[1,8,16,16,27,1]{1,5,4,3,2,0:T(2,128)(2,1)}, u32[]{:S(2)}) copy-start(bf16[1,8,16,16,27,1]{1,5,4,3,2,0:T(2,128)(2,1)} %get-tuple-element.8) | copy-start | bytes 331780
  221.1 17.2 %copy-start.1 = (bf16[1,8,16,16,27,1]{4,3,2,1,5,0:T(8,128)(2,1)S(1)}, bf16[1,8,16,16,27,1]{4,3,2,1,5,0:T(8,128)(2,1)}, u32[]{:S(2)}) copy-start(bf16[1,8,16,16,27,1]{4,3,2,1,5,0:T(8,128)(2,1)} %copy.104) | copy-start | bytes 331780
  221.1 17.8 %copy-start.2 = (bf16[1,8,16,16,27,1]{4,3,2,1,5,0:T(8,128)(2,1)S(1)}, bf16[1,8,16,16,27,1]{4,3,2,1,5,0:T(8,128)(2,1)}, u32[]{:S(2)}) copy-start(bf16[1,8,16,16,27,1]{4,3,2,1,5,0:T(8,128)(2,1)} %copy.106) | copy-start | bytes 331780
Sparse Core Ops, SparseCore 0:
  118.2 115.7 all-gather.2
where the time goes:
time: 266 us; the launch traced here: 264 us
  other arithmetic  98.5 us (37%)
  local copies, waits for them, and re-layouts  90.4 us (34%)
  waiting for transfers between devices  29.5 us (11%)
  starting transfers between devices  18.4 us (7%)
  between operations  13.7 us (5%)
  matrix products  13.6 us (5%)
    unnamed x2, other arithmetic  77.6 us
    unnamed x25, local copies, waits for them, and re-layouts  46.6 us
    another operation x2, other arithmetic  18.3 us
    all_to_all x3, local copies, waits for them, and re-layouts, per_device(): lax.all_to_all(wannier_g, 'pb', split_axis=2, concat_axis=1, tiled=True)  16.9 us
    all_gather x1, waiting for transfers between devices, per_device(): gathered = lax.all_gather(rotations, ('ka', 'pb'), axis=0, tiled=True)  12.8 us
    all_to_all x1, waiting for transfers between devices, per_device(): lax.all_to_all(lattice_sum(columns, phases), 'pb', split_axis=1, concat_a...  12.3 us
    all_to_all x1, starting transfers between devices, per_device(): lax.all_to_all(wannier_g, 'pb', split_axis=2, concat_axis=1, tiled=True)  11.6 us
    slice x1, local copies, waits for them, and re-layouts, rotate(): real_tile, imag_tile = (tiles[..., 0], tiles[..., 1])  8.69 us
  transfers between devices with their start and end apart: 3, of which 3 were waited for; matrix products, arithmetic and copies ran while one was open for 31% of the time, Pallas kernels for 0%

commit v1 on v0

v1 whole, which is shorter than its diff:
```python
import jax
import jax.numpy as jnp
from jax import lax
from jax.experimental import pallas as pl
from jax.experimental.pallas import tpu as pltpu
from jax.sharding import PartitionSpec as P

NW = 16
NKG = 8
K = 512
VEC = 54
ROWS = 30
PB = 64
KA = 8
WORKERS = 54
COLS = 256
MESH = pl.DeviceIdType.MESH
F32 = jnp.float32
BF16 = jnp.bfloat16
HALF_ROOT = 0.70703125
CUBIC = (0.5 - HALF_ROOT) / 3.0
LINEAR = HALF_ROOT - CUBIC


def worker_index(d):
    return (27 * d + 31) // 32


def is_worker(d):
    return (32 * worker_index(d)) // 27 == d


def y_step(i):
    odd = i % 2
    return odd * ((i + 1) // 2) + (1 - odd) * ((8 - i // 2) % 8)


def iota(shape, axis):
    return lax.broadcasted_iota(jnp.int32, shape, axis)


def swap_parts(x):
    width = x.shape[1]
    even = iota(x.shape, 1) % 2 == 0
    return jnp.where(even, -pltpu.roll(x, width - 1, axis=1), pltpu.roll(x, 1, axis=1))


def wave(t):
    w = (jnp.abs((t & 7) - 4) - 2).astype(F32)
    return w * (LINEAR + CUBIC * (w * w))


def comm_kernel(
    g, rot, home, shifted, lattice, blk_out, lhs1_out, lhs2_out,
    recv1, xg, acc, cosp, sinp, send2, recv2, ya, xb, zc, lat, third, lh, ll,
    g_send, g_recv, b_send, b_recv, y_send, y_recv, x_send, x_recv, z_send, z_recv, c_send, c_recv,
):
    za = lax.axis_index("ka")
    me = lax.axis_index("pb")
    yy = me // 8
    xc = me % 8
    xx = xc // 2
    cc = xc % 2
    barrier = pltpu.get_barrier_semaphore()

    def greet(s, carry):
        pl.semaphore_signal(barrier, inc=1, device_id={"pb": (me + s) % PB}, device_id_type=MESH)
        return carry

    lax.fori_loop(1, PB, greet, 0)

    def greet_z(s, carry):
        pl.semaphore_signal(barrier, inc=1, device_id={"ka": (za + s) % KA}, device_id_type=MESH)
        return carry

    lax.fori_loop(1, KA, greet_z, 0)

    lane3 = iota((3, 128), 1)
    for tile in range(16):
        a, off = (120 * tile) // 128, (120 * tile) % 128
        b = min(a + 1, 14)
        first, second = lattice[:, 128 * a : 128 * a + 128], lattice[:, 128 * b : 128 * b + 128]
        out = jnp.zeros((3, 128), jnp.int32)
        for c in range(4):
            shift = (2 * c - off) % 128
            here, there = first, second
            if shift:
                here, there = pltpu.roll(first, shift, axis=1), pltpu.roll(second, shift, axis=1)
            value = jnp.where(lane3 < 128 - off + 2 * c, here, there)
            out = jnp.where(lane3 // 32 == c, value, out)
        lat[:, 128 * tile : 128 * tile + 128] = out
    third[...] = iota((8, 2048), 0) * lat[2:3, :]
    xg[...] = jnp.zeros_like(xg)
    ya[yy] = rot[...]

    pl.semaphore_wait(barrier, PB - 1 + KA - 1)

    def y_copy(s):
        peer = (yy + s) % 8
        return pltpu.make_async_remote_copy(
            rot, ya.at[yy], y_send.at[s], y_recv.at[yy],
            device_id={"pb": peer * 8 + xc}, device_id_type=MESH)

    def y_start(s, carry):
        y_copy(s).start()
        return carry

    lax.fori_loop(1, 8, y_start, 0)

    def g_copy(d):
        cols = pl.ds(pl.multiple_of(worker_index(d) * COLS, COLS), COLS)
        return pltpu.make_async_remote_copy(
            g.at[0, :, cols], recv1.at[me], g_send.at[d], g_recv.at[me],
            device_id={"pb": d}, device_id_type=MESH)

    def g_own():
        cols = pl.ds(pl.multiple_of(worker_index(me) * COLS, COLS), COLS)
        return pltpu.make_async_copy(g.at[0, :, cols], recv1.at[me], g_recv.at[me])

    @pl.when(is_worker(me))
    def _():
        g_own().start()

    def partner(s):
        return ((yy + y_step(s // 8)) % 8) * 8 + (xc + s) % 8

    def g_start(s, carry):
        d = partner(s)

        @pl.when(is_worker(d))
        def _():
            g_copy(d).start()

        return carry

    lax.fori_loop(1, PB, g_start, 0)

    def phases(b, carry):
        first = (b // 4) * lat[0:1, :]
        second = lat[1:2, :]
        k2 = (b % 4) * 2
        low = (first + k2 * second) + third[...]
        high = (first + (k2 + 1) * second) + third[...]
        t = jnp.concatenate([low, high], axis=0)
        rows = pl.ds(pl.multiple_of(b * 16, 16), 16)
        cosp[rows, :] = wave(t).astype(BF16)
        sinp[rows, :] = wave(t + 6).astype(BF16)
        return carry

    lax.fori_loop(0, 8, phases, 0)

    def y_wait(s, carry):
        src = (yy + s) % 8
        pltpu.make_async_remote_copy(
            rot, ya.at[src], y_send.at[s], y_recv.at[src],
            device_id={"pb": src * 8 + xc}, device_id_type=MESH).wait_recv()
        return carry

    lax.fori_loop(1, 8, y_wait, 0)

    def x_copy(s, slot):
        peer = (xx + s) % 4
        return pltpu.make_async_remote_copy(
            ya, xb.at[pl.ds(8 * slot, 8)], x_send.at[s], x_recv.at[slot],
            device_id={"pb": yy * 8 + peer * 2 + cc}, device_id_type=MESH)

    for s in range(1, 4):
        x_copy(s, xx).start()
    xb[pl.ds(8 * xx, 8)] = ya[...]

    lax.fori_loop(8, 20, phases, 0)

    for s in range(1, 4):
        x_copy(s, (xx + s) % 4).wait_recv()

    def z_copy(s, slot):
        return pltpu.make_async_remote_copy(
            xb, zc.at[pl.ds((cc * 8 + slot) * 32, 32)], z_send.at[s], z_recv.at[slot],
            device_id={"ka": (za + s) % KA}, device_id_type=MESH)

    def z_start(s, carry):
        z_copy(s, za).start()
        return carry

    lax.fori_loop(1, KA, z_start, 0)
    zc[pl.ds((cc * 8 + za) * 32, 32)] = xb[...]

    lax.fori_loop(20, 32, phases, 0)

    def group(i, carry):
        ys = (yy - y_step(i) + 8) % 8

        def arrive(u, inner):
            src = ys * 8 + u

            @pl.when(src == me)
            def _():
                g_own().wait()

            @pl.when(src != me)
            def _():
                pltpu.make_async_remote_copy(
                    g.at[0, :, pl.ds(0, COLS)], recv1.at[src], g_send.at[src], g_recv.at[src],
                    device_id={"pb": src}, device_id_type=MESH).wait_recv()

            return inner

        lax.fori_loop(0, 8, arrive, 0)
        for u in range(8):
            xg[u, 0:ROWS, :] = recv1[ys * 8 + u]
        x = xg[...].reshape(256, COLS)
        x_swapped = swap_parts(x.astype(F32)).astype(BF16)
        lanes = pl.ds(pl.multiple_of(ys * 256, 256), 256)
        total = jnp.dot(cosp[:, lanes], x, preferred_element_type=F32)
        total += jnp.dot(sinp[:, lanes], x_swapped, preferred_element_type=F32)
        acc[...] += total
        return carry

    @pl.when(is_worker(me))
    def _():
        acc[...] = jnp.zeros_like(acc)
        lax.fori_loop(0, 5, group, 0)

    def z_wait(s, carry):
        z_copy(s, (za + s) % KA).wait_recv()
        return carry

    lax.fori_loop(1, KA, z_wait, 0)

    def c_copy(half):
        part = zc.at[pl.ds(half * 256, 256)]
        return pltpu.make_async_remote_copy(
            part, part, c_send.at[0], c_recv.at[0],
            device_id={"pb": me + 1 - 2 * cc}, device_id_type=MESH)

    c_copy(cc).start()

    def b_copy(d):
        return pltpu.make_async_remote_copy(
            send2.at[d], recv2.at[worker_index(me)], b_send.at[d], b_recv.at[worker_index(me)],
            device_id={"pb": d}, device_id_type=MESH)

    def b_own():
        return pltpu.make_async_copy(send2.at[me], recv2.at[worker_index(me)], b_recv.at[worker_index(me)])

    @pl.when(is_worker(me))
    def _():
        lax.fori_loop(5, 8, group, 0)

        def pack(s, carry):
            d = partner(s)
            rows = acc[pl.ds(pl.multiple_of(8 * d, 8), 8), :]
            send2[d] = jnp.concatenate([rows[:, :128], rows[:, 128:]], axis=0).astype(BF16)

            @pl.when(d != me)
            def _():
                b_copy(d).start()

            @pl.when(d == me)
            def _():
                b_own().start()

            return carry

        lax.fori_loop(0, PB, pack, 0)

    c_copy(1 - cc).wait_recv()
    r = iota((1, K), 1)
    place = (((r % 2) * 8 + r // 64) * 4 + (r // 2) % 4) * 8 + (r // 8) % 8
    sub = iota((8, K), 0)
    own = jnp.zeros((8, K), F32)
    other = jnp.zeros((8, K), F32)
    for k in range(8):
        at = jnp.minimum(jnp.sum(jnp.where(home[...] == me * 8 + k, place, 0)), K - 1)
        own = jnp.where(sub == k, zc[at], own)
        at = jnp.minimum(jnp.sum(jnp.where(home[...] == shifted[0, k], place, 0)), K - 1)
        other = jnp.where(sub == k, zc[at], other)
    both = jnp.concatenate([own, other], axis=0)
    for jp in range(32):
        pieces = [both[:, 128 * v : 128 * v + 128] for v in range(4)]
        if jp:
            pieces = [pltpu.roll(piece, 128 - jp, axis=1) for piece in pieces]
        turned = jnp.concatenate(pieces, axis=1)
        upper = turned.astype(BF16)
        lh[16 * jp : 16 * jp + 16, :] = upper
        ll[16 * jp : 16 * jp + 16, :] = (turned - upper.astype(F32)).astype(BF16)
    spread = jnp.where(iota((K, 128), 0) == 32 * (iota((K, 128), 1) // 8), 1.0, 0.0).astype(BF16)
    keep = iota((K, 128), 1) % 8 == iota((K, 128), 0) % 8
    for level, source in ((0, lh), (1, ll)):
        full = jnp.where(keep, jnp.dot(source[...], spread, preferred_element_type=F32), 0.0)
        for jj in range(8):
            for part in range(2):
                a = 16 * (4 * jj + part)
                b = 16 * (4 * jj + 2 + part)
                rows = slice(128 * level + 16 * jj, 128 * level + 16 * jj + 16)
                lanes = slice(128 * part, 128 * part + 128)
                lhs1_out[rows, lanes] = jnp.concatenate([full[a : a + 8], full[b : b + 8]], axis=0).astype(BF16)
                left = jnp.concatenate([full[a + 8 : a + 16], full[b + 8 : b + 16]], axis=0)
                lhs2_out[rows, lanes] = (left if part == 0 else -left).astype(BF16)

    def b_wait(j, carry):
        d = (32 * j) // 27

        @pl.when(d == me)
        def _():
            b_own().wait()

        @pl.when(d != me)
        def _():
            pltpu.make_async_remote_copy(
                send2.at[d], recv2.at[j], b_send.at[d], b_recv.at[j],
                device_id={"pb": d}, device_id_type=MESH).wait_recv()

        return carry

    lax.fori_loop(0, WORKERS, b_wait, 0)
    blk_out[...] = recv2[...]

    def y_left(s, carry):
        y_copy(s).wait_send()
        return carry

    lax.fori_loop(1, 8, y_left, 0)
    for s in range(1, 4):
        x_copy(s, xx).wait_send()

    def z_left(s, carry):
        z_copy(s, za).wait_send()
        return carry

    lax.fori_loop(1, KA, z_left, 0)
    c_copy(cc).wait_send()

    def g_left(s, carry):
        d = partner(s)

        @pl.when(is_worker(d))
        def _():
            g_copy(d).wait_send()

        return carry

    lax.fori_loop(1, PB, g_left, 0)

    @pl.when(is_worker(me))
    def _():
        def b_left(s, carry):
            b_copy(partner(s)).wait_send()
            return carry

        lax.fori_loop(1, PB, b_left, 0)


def rotate_kernel(blk, lhs1, lhs2, counts, out, padded, middle, final):
    lane = iota((8, 128), 1)
    low_half = lane < 64

    def compact_tile(t):
        return blk[t // 2].astype(F32)[8 * (t % 2) : 8 * (t % 2) + 8]

    tiles = [compact_tile(t) for t in range(108)]

    def turn(x, shift):
        shift %= 128
        return pltpu.roll(x, shift, axis=1) if shift else x

    for n in range(NW):
        for mp in range(8):
            halves = []
            for h in range(2):
                start = VEC * (16 * (2 * mp + h) + n)
                t, off = start // 128, start % 128
                piece = turn(tiles[t], 64 * h - off)
                if off + VEC > 128:
                    spill = turn(tiles[t + 1], 64 * h - off)
                    piece = jnp.where(lane < 128 - off + 64 * h, piece, spill)
                halves.append(piece)
            padded[8 * n : 8 * n + 8, 128 * mp : 128 * mp + 128] = jnp.where(low_half, halves[0], halves[1])

    for p in range(4):
        lanes = slice(256 * p, 256 * p + 256)
        x = padded[:, lanes]
        rhs = jnp.concatenate([x, swap_parts(x)], axis=0).astype(BF16)
        both = jnp.dot(lhs1[...], rhs, preferred_element_type=F32)
        middle[:, lanes] = both[:128] + both[128:]

    for a in range(8):
        for b in range(8):
            lanes = slice(128 * b, 128 * b + 128)
            first = middle[16 * a : 16 * a + 8, lanes]
            second = middle[16 * a + 8 : 16 * a + 16, lanes]
            place = slice(128 * a, 128 * a + 128)
            padded[16 * b : 16 * b + 8, place] = jnp.where(low_half, first, turn(second, 64))
            padded[16 * b + 8 : 16 * b + 16, place] = jnp.where(low_half, turn(first, 64), second)

    sub = iota((8, 1), 0)
    limit = jnp.zeros((8, 1), jnp.int32)
    for k in range(8):
        limit = jnp.where(sub == k, counts[0, k], limit)
    row = iota((128, 256), 0)
    limits = jnp.concatenate([jnp.broadcast_to(limit, (8, 256))] * 16, axis=0)
    for p in range(4):
        lanes = slice(256 * p, 256 * p + 256)
        x = padded[:, lanes]
        x = jnp.concatenate([x, swap_parts(x)], axis=0)
        upper = x.astype(BF16)
        lower = (x - upper.astype(F32)).astype(BF16)
        both = jnp.dot(lhs2[...], upper, preferred_element_type=F32)
        total = both[:128] + (both[128:] + jnp.dot(lhs2[:128, :], lower, preferred_element_type=F32))
        band = jnp.maximum(row // 8, 4 * p + iota((128, 256), 1) // 64)
        final[:, lanes] = jnp.where(band < limits, total, 0.0)

    for t in range(108):
        begin = 128 * t
        value = None
        for q in range(begin // VEC, (begin + 127) // VEC + 1):
            if q >= 256:
                continue
            i, j = q // 16, q % 16
            at = VEC * q - begin
            piece = turn(final[8 * i : 8 * i + 8, 128 * (j // 2) : 128 * (j // 2) + 128], at - 64 * (j % 2))
            value = piece if value is None else jnp.where(lane < at, value, piece)
        out[0, :, begin : begin + 128] = value.astype(BF16)


def per_device(wannier_g, rotations, home_rows, shifted, band_count, lattice):
    vmem = pl.BlockSpec(memory_space=pltpu.VMEM)
    smem = pl.BlockSpec(memory_space=pltpu.SMEM)
    dma = pltpu.SemaphoreType.DMA
    blocks, lhs1, lhs2 = pl.pallas_call(
        comm_kernel,
        out_shape=(
            jax.ShapeDtypeStruct((WORKERS, 16, 128), BF16),
            jax.ShapeDtypeStruct((256, 256), BF16),
            jax.ShapeDtypeStruct((256, 256), BF16),
        ),
        in_specs=[pl.BlockSpec(memory_space=pl.ANY), vmem, vmem, smem, vmem],
        out_specs=(vmem, vmem, vmem),
        scratch_shapes=[
            pltpu.VMEM((PB, ROWS, COLS), BF16),
            pltpu.VMEM((8, 32, COLS), BF16),
            pltpu.VMEM((K, COLS), F32),
            pltpu.VMEM((K, 2048), BF16),
            pltpu.VMEM((K, 2048), BF16),
            pltpu.VMEM((PB, 16, 128), BF16),
            pltpu.VMEM((WORKERS, 16, 128), BF16),
            pltpu.VMEM((8, 1, 512), F32),
            pltpu.VMEM((32, 1, 512), F32),
            pltpu.VMEM((512, 1, 512), F32),
            pltpu.VMEM((3, 2048), jnp.int32),
            pltpu.VMEM((8, 2048), jnp.int32),
            pltpu.VMEM((K, 512), BF16),
            pltpu.VMEM((K, 512), BF16),
            dma((PB,)), dma((PB,)), dma((PB,)), dma((WORKERS,)),
            dma((8,)), dma((8,)), dma((4,)), dma((4,)), dma((8,)), dma((8,)), dma((1,)), dma((1,)),
        ],
        compiler_params=pltpu.CompilerParams(
            collective_id=0, has_side_effects=True, vmem_limit_bytes=40 * 1024 * 1024
        ),
        name="exchange",
    )(wannier_g, rotations, home_rows.reshape(1, K), shifted, lattice)
    return pl.pallas_call(
        rotate_kernel,
        out_shape=jax.ShapeDtypeStruct((1, 8, NW * NW * VEC), BF16),
        in_specs=[vmem, vmem, vmem, smem],
        out_specs=vmem,
        scratch_shapes=[
            pltpu.VMEM((128, 1024), F32),
            pltpu.VMEM((128, 1024), F32),
            pltpu.VMEM((128, 1024), F32),
        ],
        compiler_params=pltpu.CompilerParams(vmem_limit_bytes=32 * 1024 * 1024),
        name="rotate",
    )(blocks, lhs1, lhs2, band_count)


def solution(mesh):
    placed = (P("ka", "pb", None), P(("ka", "pb"), None), P(), P("ka", "pb"), P("ka", "pb"), P())
    return jax.shard_map(
        per_device, mesh=mesh, in_specs=placed, out_specs=P("ka", "pb", None), check_vma=False
    )
```

time: 266 us -> 66.2 us (0.25)
  other arithmetic: 98.5 us -> 0 us
  local copies, waits for them, and re-layouts: 90.4 us -> 4.59 us
  Pallas kernels: 0 us -> 61.3 us
  waiting for transfers between devices: 29.5 us -> 0 us
  starting transfers between devices: 18.4 us -> 0 us
  between operations: 13.7 us -> 0.02 us
  matrix products: 13.6 us -> 0 us
    unnamed x2 -> x0, other arithmetic: 77.6 us -> none
    pallas_call x0 -> x2, Pallas kernels: none -> 61.3 us  [the longest x1 58.6 us: per_device(): pl.pallas_call(comm_kernel, out_shape=(jax.ShapeDtypeStruct((WORKERS, 16,...]
    unnamed x25 -> x12, local copies, waits for them, and re-layouts: 46.6 us -> 4.59 us
    all_to_all x4 -> x0, local copies, waits for them, and re-layouts: 20.2 us -> none  [the longest x3 16.9 us: per_device(): lax.all_to_all(wannier_g, 'pb', split_axis=2, concat_axis=1, tiled=True)]
    another operation x4 -> x0, other arithmetic: 20 us -> none
    all_to_all x2 -> x0, starting transfers between devices: 18.1 us -> none  [the longest x1 11.6 us: per_device(): lax.all_to_all(wannier_g, 'pb', split_axis=2, concat_axis=1, tiled=True)]
    all_to_all x2 -> x0, waiting for transfers between devices: 16.1 us -> none  [the longest x1 12.3 us: per_device(): lax.all_to_all(lattice_sum(columns, phases), 'pb', split_axis=1, concat_a...]
    dot_general x10 -> x0, matrix products: 13.6 us -> none  [the longest x8 8.32 us: contract(): jnp.einsum(form, first_op, second_op, precision=lax.Precision.HIGHEST)]
  transfers between devices with their start and end apart: 3 -> 0, of which waited for: 3 -> 0; matrix products, arithmetic and copies ran while one was open for 31% -> 0% of each run, Pallas kernels for 0% -> 0%
where the time goes in v1:
time: 66.2 us; the launch traced here: 65.9 us
  Pallas kernels  61.3 us (93%)
  local copies, waits for them, and re-layouts  4.59 us (7%)
    pallas_call x1, Pallas kernels, per_device(): pl.pallas_call(comm_kernel, out_shape=(jax.ShapeDtypeStruct((WORKERS, 16,...  58.6 us
    unnamed x12, local copies, waits for them, and re-layouts  4.59 us
    pallas_call x1, Pallas kernels, per_device(): pl.pallas_call(rotate_kernel, out_shape=jax.ShapeDtypeStruct((1, 8, NW *...  2.7 us

profile of v1, /device:TPU:1, one launch (start us, length us, event | category | flops | bytes accessed | tf_op | source)
XLA Modules:
  0.0 65.9 jit_solution(15203206008270798872)
XLA Ops:
  0.0 0.0 copy-start.4
  0.0 0.7 copy-done.4
  0.7 0.0 copy-start
  0.7 1.2 %copy-done = bf16[1,30,13824]{2,1,0:T(8,128)(2,1)S(1)} copy-done((bf16[1,30,13824]{2,1,0:T(8,128)(2,1)S(1)}, bf16[1,30,13824]{2,1,0:T(8,128)(2,1)}, u32[]{:S(2)}) %copy-start) | copy-done | bytes 829464
  1.8 0.0 copy-start.1
  1.8 0.8 %copy-done.1 = s32[3,1920]{1,0:T(4,128)S(1)} copy-done((s32[3,1920]{1,0:T(4,128)S(1)}, s32[3,1920]{1,0:T(4,128)}, u32[]{:S(2)}) %copy-start.1) | copy-done | bytes 23064
  2.6 0.0 copy-start.2
  2.6 0.7 %copy-done.2 = f32[1,512]{1,0:T(1,128)S(1)} copy-done((f32[1,512]{1,0:T(1,128)S(1)}, f32[1,512]{1,0:T(1,128)}, u32[]{:S(2)}) %copy-start.2) | copy-done | bytes 2072
  3.3 0.0 copy-start.3
  3.3 0.7 %copy-done.3 = s32[512]{0:T(512)S(1)} copy-done((s32[512]{0:T(512)S(1)}, s32[512]{0:T(512)}, u32[]{:S(2)}) %copy-start.3) | copy-done | bytes 2072
  3.9 58.6 %exchange.1 = (bf16[54,16,128]{2,1,0:T(8,128)(2,1)S(1)}, bf16[256,256]{1,0:T(8,128)(2,1)S(1)}, bf16[256,256]{1,0:T(8,128)(2,1)S(1)}) custom-call(bf16[1,30,13824]{2,1,0:T(8,128)(2,1)S(1)} %copy-done, f32[1,512]{1,0:T(1,128)S(1)} %copy-done.2, s32[1,512]{1,0:T(1,128)S(1)} %bitcast.1, s32[1,8]{1,0:T(1,128)S(1)} %copy-done.4, s32[3,1920]{1,0:T(4,128)S(1)} %copy-done.1), custom_call_target="tpu_custom_call" | custom-call | tf_op jit(solution)/shard_map/exchange/pallas_call | solution.py:430
  62.6 0.0 copy-start.5
  62.6 0.6 copy-done.5
  63.2 2.7 %rotate.1 = bf16[1,8,13824]{2,1,0:T(8,128)(2,1)} custom-call(bf16[54,16,128]{2,1,0:T(8,128)(2,1)S(1)} %get-tuple-element.8.blk, bf16[256,256]{1,0:T(8,128)(2,1)S(1)} %get-tuple-element.9.lhs1, bf16[256,256]{1,0:T(8,128)(2,1)S(1)} %get-tuple-element.10.lhs2, s32[1,8]{1,0:T(1,128)S(1)} %copy-done.5), custom_call_target="tpu_custom_call" | custom-call | tf_op jit(solution)/shard_map/rotate/pallas_call | solution.py:462
Async XLA Ops:
  0.0 0.7 copy-start.4
  0.7 1.2 %copy-start = (bf16[1,30,13824]{2,1,0:T(8,128)(2,1)S(1)}, bf16[1,30,13824]{2,1,0:T(8,128)(2,1)}, u32[]{:S(2)}) copy-start(bf16[1,30,13824]{2,1,0:T(8,128)(2,1)} %g.1) | copy-start | bytes 2488324
  1.8 0.8 %copy-start.1 = (s32[3,1920]{1,0:T(4,128)S(1)}, s32[3,1920]{1,0:T(4,128)}, u32[]{:S(2)}) copy-start(s32[3,1920]{1,0:T(4,128)} %lattice.1) | copy-start | bytes 69124
  2.6 0.7 %copy-start.2 = (f32[1,512]{1,0:T(1,128)S(1)}, f32[1,512]{1,0:T(1,128)}, u32[]{:S(2)}) copy-start(f32[1,512]{1,0:T(1,128)} %rot.1) | copy-start | bytes 6148
  3.3 0.7 %copy-start.3 = (s32[512]{0:T(512)S(1)}, s32[512]{0:T(512)}, u32[]{:S(2)}) copy-start(s32[512]{0:T(512)} %param.8) | copy-start | bytes 6148
  62.6 0.7 copy-start.5

commit v2 on v1

v2 whole, which is shorter than its diff:
```python
import jax
import jax.numpy as jnp
from jax import lax
from jax.experimental import pallas as pl
from jax.experimental.pallas import tpu as pltpu
from jax.sharding import PartitionSpec as P

NW = 16
NKG = 8
K = 512
VEC = 54
ROWS = 30
PB = 64
KA = 8
Y_ORDER = (0, 1, 7, 2, 6, 3, 5, 4)
WORKERS = 54
COLS = 256
MESH = pl.DeviceIdType.MESH
F32 = jnp.float32
BF16 = jnp.bfloat16
HALF_ROOT = 0.70703125
CUBIC = (0.5 - HALF_ROOT) / 3.0
LINEAR = HALF_ROOT - CUBIC


def worker_index(d):
    return (27 * d + 31) >> 5


def is_worker(d):
    return ((5 * d) & 31) < 27


def iota(shape, axis):
    return lax.broadcasted_iota(jnp.int32, shape, axis)


def swap_parts(x):
    width = x.shape[1]
    even = iota(x.shape, 1) % 2 == 0
    return jnp.where(even, -pltpu.roll(x, width - 1, axis=1), pltpu.roll(x, 1, axis=1))


def wave(t):
    w = (jnp.abs((t & 7) - 4) - 2).astype(F32)
    return w * (LINEAR + CUBIC * (w * w))


def comm_kernel(
    g, rot_hbm, home_hbm, shifted_hbm, lattice_hbm, blk_out, lhs1_out, lhs2_out,
    rot, home, shifted, lattice, recv1, xg, acc, cosp, sinp, send2, ya, xb, zc, lat, third, lh, ll, lhs1, lhs2,
    in_sem, g_send, g_recv, b_send, b_recv, y_send, y_recv, x_send, x_recv, z_send, z_recv, c_send, c_recv, out_sem,
):
    za = lax.axis_index("ka")
    me = lax.axis_index("pb")
    yy = me >> 3
    xc = me & 7
    xx = xc >> 1
    cc = xc & 1
    working = is_worker(me)
    barrier = pltpu.get_barrier_semaphore()
    reads = [
        pltpu.make_async_copy(source, target, in_sem.at[i])
        for i, (source, target) in enumerate(
            ((lattice_hbm, lattice), (rot_hbm, rot), (home_hbm, home), (shifted_hbm, shifted)))
    ]
    for read in reads:
        read.start()

    def greet(s, carry):
        pl.semaphore_signal(barrier, inc=1, device_id=(za, me ^ s), device_id_type=MESH)
        return carry

    lax.fori_loop(1, PB, greet, 0)

    def greet_z(s, carry):
        pl.semaphore_signal(barrier, inc=1, device_id=(za ^ s, me), device_id_type=MESH)
        return carry

    lax.fori_loop(1, KA, greet_z, 0)

    for read in reads:
        read.wait()

    lane3 = iota((3, 128), 1)
    for tile in range(16):
        a, off = (120 * tile) // 128, (120 * tile) % 128
        b = min(a + 1, 14)
        first, second = lattice[:, 128 * a : 128 * a + 128], lattice[:, 128 * b : 128 * b + 128]
        out = jnp.zeros((3, 128), jnp.int32)
        for c in range(4):
            shift = (2 * c - off) % 128
            here, there = first, second
            if shift:
                here, there = pltpu.roll(first, shift, axis=1), pltpu.roll(second, shift, axis=1)
            value = jnp.where(lane3 < 128 - off + 2 * c, here, there)
            out = jnp.where(lane3 // 32 == c, value, out)
        lat[:, 128 * tile : 128 * tile + 128] = out
    third[...] = iota((8, 2048), 0) * lat[2:3, :]
    xg[...] = jnp.zeros_like(xg)
    ya[yy] = rot[...]

    def phases(b, carry):
        first = (b >> 2) * lat[0:1, :]
        second = lat[1:2, :]
        k2 = (b & 3) * 2
        low = (first + k2 * second) + third[...]
        high = (first + (k2 + 1) * second) + third[...]
        t = jnp.concatenate([low, high], axis=0)
        rows = pl.ds(pl.multiple_of(b * 16, 16), 16)
        cosp[rows, :] = wave(t).astype(BF16)
        sinp[rows, :] = wave(t + 6).astype(BF16)
        return carry

    pl.semaphore_wait(barrier, PB - 1 + KA - 1)

    def y_copy(s):
        peer = (yy + s) & 7
        return pltpu.make_async_remote_copy(
            rot, ya.at[yy], y_send.at[s], y_recv.at[yy],
            device_id=(za, peer * 8 + xc), device_id_type=MESH)

    def y_start(s, carry):
        y_copy(s).start()
        return carry

    lax.fori_loop(1, 8, y_start, 0)

    def g_columns(d):
        return g.at[0, :, pl.ds(pl.multiple_of(worker_index(d) * COLS, COLS), COLS)]

    @pl.when(working)
    def _():
        pltpu.make_async_copy(g_columns(me), recv1.at[me], g_recv.at[yy]).start()

    def g_start(step):
        base = ((yy + step) & 7) * 8

        def one(u, carry):
            d = base + (xc ^ u)

            @pl.when(is_worker(d))
            def _():
                pltpu.make_async_remote_copy(
                    g_columns(d), recv1.at[me], g_send.at[0], g_recv.at[yy],
                    device_id=(za, d), device_id_type=MESH).start()

            return carry

        lax.fori_loop(0 if step else 1, 8, one, 0)

    for step in Y_ORDER[:1]:
        g_start(step)

    lax.fori_loop(0, 8, phases, 0)

    def y_wait(s, carry):
        src = (yy + s) & 7
        pltpu.make_async_remote_copy(
            rot, ya.at[src], y_send.at[s], y_recv.at[src],
            device_id=(za, src * 8 + xc), device_id_type=MESH).wait_recv()
        return carry

    lax.fori_loop(1, 8, y_wait, 0)

    def x_copy(s, slot):
        peer = (xx + s) & 3
        return pltpu.make_async_remote_copy(
            ya, xb.at[pl.ds(8 * slot, 8)], x_send.at[s], x_recv.at[slot],
            device_id=(za, yy * 8 + peer * 2 + cc), device_id_type=MESH)

    for s in range(1, 4):
        x_copy(s, xx).start()
    xb[pl.ds(8 * xx, 8)] = ya[...]

    for step in Y_ORDER[1:3]:
        g_start(step)
    lax.fori_loop(8, 20, phases, 0)

    for s in range(1, 4):
        x_copy(s, (xx + s) & 3).wait_recv()

    def z_copy(s, slot):
        return pltpu.make_async_remote_copy(
            xb, zc.at[pl.ds((cc * 8 + slot) * 32, 32)], z_send.at[s], z_recv.at[slot],
            device_id=((za + s) & 7, me), device_id_type=MESH)

    def z_start(s, carry):
        z_copy(s, za).start()
        return carry

    lax.fori_loop(1, KA, z_start, 0)
    zc[pl.ds((cc * 8 + za) * 32, 32)] = xb[...]

    for step in Y_ORDER[3:]:
        g_start(step)
    lax.fori_loop(20, 32, phases, 0)

    def group(step):
        ys = (yy - step) & 7
        arrived = recv1.at[pl.ds(8 * ys, 8)]
        pltpu.make_async_copy(arrived, arrived, g_recv.at[ys]).wait()
        for u in range(8):
            xg[u, 0:ROWS, :] = recv1[ys * 8 + u]
        x = xg[...].reshape(256, COLS)
        x_swapped = swap_parts(x.astype(F32)).astype(BF16)
        lanes = pl.ds(pl.multiple_of(ys * 256, 256), 256)
        total = jnp.dot(cosp[:, lanes], x, preferred_element_type=F32)
        total += jnp.dot(sinp[:, lanes], x_swapped, preferred_element_type=F32)
        if step == 0:
            acc[...] = total
        else:
            acc[...] += total

    @pl.when(working)
    def _():
        for step in Y_ORDER[:5]:
            group(step)

    def z_wait(s, carry):
        z_copy(s, (za + s) & 7).wait_recv()
        return carry

    lax.fori_loop(1, KA, z_wait, 0)

    def c_copy(half):
        part = zc.at[pl.ds(half * 256, 256)]
        return pltpu.make_async_remote_copy(
            part, part, c_send.at[0], c_recv.at[0], device_id=(za, me ^ 1), device_id_type=MESH)

    c_copy(cc).start()

    @pl.when(working)
    def _():
        for step in Y_ORDER[5:]:
            group(step)
        slot = worker_index(me)

        def pack(s, carry):
            d = me ^ s
            rows = acc[pl.ds(pl.multiple_of(8 * d, 8), 8), :]
            send2[d] = jnp.concatenate([rows[:, :128], rows[:, 128:]], axis=0).astype(BF16)

            @pl.when(s > 0)
            def _():
                pltpu.make_async_remote_copy(
                    send2.at[d], blk_out.at[slot], b_send.at[0], b_recv.at[0],
                    device_id=(za, d), device_id_type=MESH).start()

            return carry

        lax.fori_loop(0, PB, pack, 0)
        pltpu.make_async_copy(send2.at[me], blk_out.at[slot], b_recv.at[0]).start()

    c_copy(1 - cc).wait_recv()
    r = iota((1, K), 1)
    place = (((r & 1) * 8 + (r >> 6)) * 4 + ((r >> 1) & 3)) * 8 + ((r >> 3) & 7)
    sub = iota((8, K), 0)
    own = jnp.zeros((8, K), F32)
    other = jnp.zeros((8, K), F32)
    for k in range(8):
        at = jnp.minimum(jnp.sum(jnp.where(home[...] == me * 8 + k, place, 0)), K - 1)
        own = jnp.where(sub == k, zc[at], own)
        at = jnp.minimum(jnp.sum(jnp.where(home[...] == shifted[0, k], place, 0)), K - 1)
        other = jnp.where(sub == k, zc[at], other)
    both = jnp.concatenate([own, other], axis=0)
    for jp in range(32):
        pieces = [both[:, 128 * v : 128 * v + 128] for v in range(4)]
        if jp:
            pieces = [pltpu.roll(piece, 128 - jp, axis=1) for piece in pieces]
        turned = jnp.concatenate(pieces, axis=1)
        upper = turned.astype(BF16)
        lh[16 * jp : 16 * jp + 16, :] = upper
        ll[16 * jp : 16 * jp + 16, :] = (turned - upper.astype(F32)).astype(BF16)
    spread = jnp.where(iota((K, 128), 0) == 32 * (iota((K, 128), 1) // 8), 1.0, 0.0).astype(BF16)
    keep = iota((K, 128), 1) % 8 == iota((K, 128), 0) % 8
    for level, source in ((0, lh), (1, ll)):
        full = jnp.where(keep, jnp.dot(source[...], spread, preferred_element_type=F32), 0.0)
        for jj in range(8):
            for part in range(2):
                a = 16 * (4 * jj + part)
                b = 16 * (4 * jj + 2 + part)
                rows = slice(128 * level + 16 * jj, 128 * level + 16 * jj + 16)
                lanes = slice(128 * part, 128 * part + 128)
                lhs1[rows, lanes] = jnp.concatenate([full[a : a + 8], full[b : b + 8]], axis=0).astype(BF16)
                left = jnp.concatenate([full[a + 8 : a + 16], full[b + 8 : b + 16]], axis=0)
                lhs2[rows, lanes] = (left if part == 0 else -left).astype(BF16)
    outs = [pltpu.make_async_copy(lhs1, lhs1_out, out_sem.at[0]), pltpu.make_async_copy(lhs2, lhs2_out, out_sem.at[1])]
    for out in outs:
        out.start()

    def y_left(s, carry):
        y_copy(s).wait_send()
        return carry

    lax.fori_loop(1, 8, y_left, 0)
    for s in range(1, 4):
        x_copy(s, xx).wait_send()

    def z_left(s, carry):
        z_copy(s, za).wait_send()
        return carry

    lax.fori_loop(1, KA, z_left, 0)
    c_copy(cc).wait_send()

    @pl.when(working)
    def _():
        sent = recv1.at[pl.ds(0, WORKERS - 1)]
        pltpu.make_async_copy(sent, sent, g_send.at[0]).wait()
        sent = send2.at[pl.ds(0, PB - 1)]
        pltpu.make_async_copy(sent, sent, b_send.at[0]).wait()

    @pl.when(jnp.logical_not(working))
    def _():
        sent = recv1.at[pl.ds(0, WORKERS)]
        pltpu.make_async_copy(sent, sent, g_send.at[0]).wait()

    for out in outs:
        out.wait()
    pltpu.make_async_copy(blk_out, blk_out, b_recv.at[0]).wait()


def rotate_kernel(
    blk_hbm, lhs1_hbm, lhs2_hbm, counts_hbm, out, blk, lhs1, lhs2, counts, padded, middle, final, in_sem
):
    reads = [
        pltpu.make_async_copy(source, target, in_sem.at[i])
        for i, (source, target) in enumerate(
            ((blk_hbm, blk), (lhs1_hbm, lhs1), (lhs2_hbm, lhs2), (counts_hbm, counts)))
    ]
    for read in reads:
        read.start()
    lane = iota((8, 128), 1)
    low_half = lane < 64

    def compact_tile(t):
        return blk[t // 2].astype(F32)[8 * (t % 2) : 8 * (t % 2) + 8]

    reads[0].wait()
    tiles = [compact_tile(t) for t in range(108)]

    def turn(x, shift):
        shift %= 128
        return pltpu.roll(x, shift, axis=1) if shift else x

    for n in range(NW):
        for mp in range(8):
            halves = []
            for h in range(2):
                start = VEC * (16 * (2 * mp + h) + n)
                t, off = start // 128, start % 128
                piece = turn(tiles[t], 64 * h - off)
                if off + VEC > 128:
                    spill = turn(tiles[t + 1], 64 * h - off)
                    piece = jnp.where(lane < 128 - off + 64 * h, piece, spill)
                halves.append(piece)
            padded[8 * n : 8 * n + 8, 128 * mp : 128 * mp + 128] = jnp.where(low_half, halves[0], halves[1])

    reads[1].wait()
    for p in range(4):
        lanes = slice(256 * p, 256 * p + 256)
        x = padded[:, lanes]
        rhs = jnp.concatenate([x, swap_parts(x)], axis=0).astype(BF16)
        both = jnp.dot(lhs1[...], rhs, preferred_element_type=F32)
        middle[:, lanes] = both[:128] + both[128:]

    for a in range(8):
        for b in range(8):
            lanes = slice(128 * b, 128 * b + 128)
            first = middle[16 * a : 16 * a + 8, lanes]
            second = middle[16 * a + 8 : 16 * a + 16, lanes]
            place = slice(128 * a, 128 * a + 128)
            padded[16 * b : 16 * b + 8, place] = jnp.where(low_half, first, turn(second, 64))
            padded[16 * b + 8 : 16 * b + 16, place] = jnp.where(low_half, turn(first, 64), second)

    reads[2].wait()
    reads[3].wait()
    sub = iota((8, 1), 0)
    limit = jnp.zeros((8, 1), jnp.int32)
    for k in range(8):
        limit = jnp.where(sub == k, counts[0, k], limit)
    row = iota((128, 256), 0)
    limits = jnp.concatenate([jnp.broadcast_to(limit, (8, 256))] * 16, axis=0)
    for p in range(4):
        lanes = slice(256 * p, 256 * p + 256)
        x = padded[:, lanes]
        x = jnp.concatenate([x, swap_parts(x)], axis=0)
        upper = x.astype(BF16)
        lower = (x - upper.astype(F32)).astype(BF16)
        both = jnp.dot(lhs2[...], upper, preferred_element_type=F32)
        total = both[:128] + (both[128:] + jnp.dot(lhs2[:128, :], lower, preferred_element_type=F32))
        band = jnp.maximum(row // 8, 4 * p + iota((128, 256), 1) // 64)
        final[:, lanes] = jnp.where(band < limits, total, 0.0)

    for t in range(108):
        begin = 128 * t
        value = None
        for q in range(begin // VEC, (begin + 127) // VEC + 1):
            if q >= 256:
                continue
            i, j = q // 16, q % 16
            at = VEC * q - begin
            piece = turn(final[8 * i : 8 * i + 8, 128 * (j // 2) : 128 * (j // 2) + 128], at - 64 * (j % 2))
            value = piece if value is None else jnp.where(lane < at, value, piece)
        out[0, :, begin : begin + 128] = value.astype(BF16)


def per_device(wannier_g, rotations, home_rows, shifted, band_count, lattice):
    vmem = pl.BlockSpec(memory_space=pltpu.VMEM)
    hbm = pl.BlockSpec(memory_space=pltpu.HBM)
    dma = pltpu.SemaphoreType.DMA
    blocks, lhs1, lhs2 = pl.pallas_call(
        comm_kernel,
        out_shape=(
            jax.ShapeDtypeStruct((WORKERS, 16, 128), BF16),
            jax.ShapeDtypeStruct((256, 256), BF16),
            jax.ShapeDtypeStruct((256, 256), BF16),
        ),
        in_specs=[hbm] * 5,
        out_specs=(hbm, hbm, hbm),
        scratch_shapes=[
            pltpu.VMEM((1, K), F32),
            pltpu.VMEM((1, K), jnp.int32),
            pltpu.SMEM((1, 8), jnp.int32),
            pltpu.VMEM((3, 1920), jnp.int32),
            pltpu.VMEM((PB, ROWS, COLS), BF16),
            pltpu.VMEM((8, 32, COLS), BF16),
            pltpu.VMEM((K, COLS), F32),
            pltpu.VMEM((K, 2048), BF16),
            pltpu.VMEM((K, 2048), BF16),
            pltpu.VMEM((PB, 16, 128), BF16),
            pltpu.VMEM((8, 1, 512), F32),
            pltpu.VMEM((32, 1, 512), F32),
            pltpu.VMEM((512, 1, 512), F32),
            pltpu.VMEM((3, 2048), jnp.int32),
            pltpu.VMEM((8, 2048), jnp.int32),
            pltpu.VMEM((K, 512), BF16),
            pltpu.VMEM((K, 512), BF16),
            pltpu.VMEM((256, 256), BF16),
            pltpu.VMEM((256, 256), BF16),
            dma((4,)), dma((1,)), dma((8,)), dma((1,)), dma((1,)),
            dma((8,)), dma((8,)), dma((4,)), dma((4,)), dma((8,)), dma((8,)), dma((1,)), dma((1,)), dma((2,)),
        ],
        compiler_params=pltpu.CompilerParams(
            collective_id=0, has_side_effects=True, vmem_limit_bytes=60 * 1024 * 1024
        ),
        name="exchange",
    )(wannier_g, rotations, home_rows.reshape(1, K), shifted, lattice)
    return pl.pallas_call(
        rotate_kernel,
        out_shape=jax.ShapeDtypeStruct((1, 8, NW * NW * VEC), BF16),
        in_specs=[hbm] * 4,
        out_specs=vmem,
        scratch_shapes=[
            pltpu.VMEM((WORKERS, 16, 128), BF16),
            pltpu.VMEM((256, 256), BF16),
            pltpu.VMEM((256, 256), BF16),
            pltpu.SMEM((1, 8), jnp.int32),
            pltpu.VMEM((128, 1024), F32),
            pltpu.VMEM((128, 1024), F32),
            pltpu.VMEM((128, 1024), F32),
            dma((4,)),
        ],
        compiler_params=pltpu.CompilerParams(vmem_limit_bytes=60 * 1024 * 1024),
        name="rotate",
    )(blocks, lhs1, lhs2, band_count)


def solution(mesh):
    placed = (P("ka", "pb", None), P(("ka", "pb"), None), P(), P("ka", "pb"), P("ka", "pb"), P())
    return jax.shard_map(
        per_device, mesh=mesh, in_specs=placed, out_specs=P("ka", "pb", None), check_vma=False
    )
```

time: 66.2 us -> 56.9 us (0.86)
  Pallas kernels: 61.3 us -> 56.7 us
  local copies, waits for them, and re-layouts: 4.59 us -> 0 us
    pallas_call x1, Pallas kernels: 58.6 us -> 53.5 us  [per_device(): pl.pallas_call(comm_kernel, out_shape=(jax.ShapeDtypeStruct((WORKERS, 16,...]
    unnamed x12 -> x0, local copies, waits for them, and re-layouts: 4.59 us -> none
where the time goes in v2:
time: 56.9 us; the launch traced here: 56.7 us
  Pallas kernels  56.7 us (100%)
    pallas_call x1, Pallas kernels, per_device(): pl.pallas_call(comm_kernel, out_shape=(jax.ShapeDtypeStruct((WORKERS, 16,...  53.5 us
    pallas_call x1, Pallas kernels, per_device(): pl.pallas_call(rotate_kernel, out_shape=jax.ShapeDtypeStruct((1, 8, NW *...  3.26 us

profile of v2, /device:TPU:1, one launch (start us, length us, event | category | flops | bytes accessed | tf_op | source)
XLA Modules:
  0.0 56.7 jit_solution(7924527282420799661)
XLA Ops:
  0.0 53.5 %exchange.1 = (bf16[54,16,128]{2,1,0:T(8,128)(2,1)}, bf16[256,256]{1,0:T(8,128)(2,1)}, bf16[256,256]{1,0:T(8,128)(2,1)}) custom-call(bf16[1,30,13824]{2,1,0:T(8,128)(2,1)} %g.1, f32[1,512]{1,0:T(1,128)} %rot_hbm.1, s32[1,512]{1,0:T(1,128)} %bitcast.1, s32[1,8]{1,0:T(1,128)} %shifted_hbm.1, s32[3,1920]{1,0:T(4,128)} %lattice_hbm.1), custom_call_target="tpu_custom_call" | custom-call | tf_op jit(solution)/shard_map/exchange/pallas_call | solution.py:413
  53.5 3.3 %rotate.1 = bf16[1,8,13824]{2,1,0:T(8,128)(2,1)} custom-call(bf16[54,16,128]{2,1,0:T(8,128)(2,1)} %get-tuple-element.8.blk_hbm, bf16[256,256]{1,0:T(8,128)(2,1)} %get-tuple-element.9.lhs1_hbm, bf16[256,256]{1,0:T(8,128)(2,1)} %get-tuple-element.10.lhs2_hbm, s32[1,8]{1,0:T(1,128)} %counts_hbm.1), custom_call_target="tpu_custom_call" | custom-call | tf_op jit(solution)/shard_map/rotate/pallas_call | solution.py:450

commit v3 on v2

--- a/solution.py
+++ b/solution.py
@@ -12,7 +12,9 @@
 ROWS = 30
 PB = 64
 KA = 8
-Y_ORDER = (0, 1, 7, 2, 6, 3, 5, 4)
+Y_ORDER = (1, 7, 2, 6, 3, 5, 4, 0)
+EARLY = 4
+MIDDLE = 4
 WORKERS = 54
 COLS = 256
 MESH = pl.DeviceIdType.MESH
@@ -48,7 +50,7 @@
 
 def comm_kernel(
     g, rot_hbm, home_hbm, shifted_hbm, lattice_hbm, blk_out, lhs1_out, lhs2_out,
-    rot, home, shifted, lattice, recv1, xg, acc, cosp, sinp, send2, ya, xb, zc, lat, third, lh, ll, lhs1, lhs2,
+    home, shifted, lattice, recv1, xg, acc, cosp, sinp, send2, ya, xb, zc, lat, third, lh, ll, lhs1, lhs2,
     in_sem, g_send, g_recv, b_send, b_recv, y_send, y_recv, x_send, x_recv, z_send, z_recv, c_send, c_recv, out_sem,
 ):
     za = lax.axis_index("ka")
@@ -62,7 +64,7 @@
     reads = [
         pltpu.make_async_copy(source, target, in_sem.at[i])
         for i, (source, target) in enumerate(
-            ((lattice_hbm, lattice), (rot_hbm, rot), (home_hbm, home), (shifted_hbm, shifted)))
+            ((lattice_hbm, lattice), (rot_hbm, ya.at[yy]), (home_hbm, home), (shifted_hbm, shifted)))
     ]
     for read in reads:
         read.start()
@@ -79,8 +81,70 @@
 
     lax.fori_loop(1, KA, greet_z, 0)
 
-    for read in reads:
+    pl.semaphore_wait(barrier, PB - 1 + KA - 1)
+
+    def y_copy(s):
+        peer = (yy + s) & 7
+        return pltpu.make_async_remote_copy(
+            rot_hbm, ya.at[yy], y_send.at[s], y_recv.at[yy],
+            device_id=(za, peer * 8 + xc), device_id_type=MESH)
+
+    def y_start(s, carry):
+        y_copy(s).start()
+        return carry
+
+    lax.fori_loop(1, 8, y_start, 0)
+
+    def g_columns(d):
+        return g.at[0, :, pl.ds(pl.multiple_of(worker_index(d) * COLS, COLS), COLS)]
+
+    @pl.when(working)
+    def _():
+        pltpu.make_async_copy(g_columns(me), recv1.at[me], g_recv.at[yy]).start()
+
+    def g_start(step):
+        base = ((yy + step) & 7) * 8
+
+        def one(u, carry):
+            d = base + (xc ^ u)
+
+            @pl.when(is_worker(d))
+            def _():
+                pltpu.make_async_remote_copy(
+                    g_columns(d), recv1.at[me], g_send.at[0], g_recv.at[yy],
+                    device_id=(za, d), device_id_type=MESH).start()
+
+            return carry
+
+        lax.fori_loop(0 if step else 1, 8, one, 0)
+
+    for step in Y_ORDER[:EARLY]:
+        g_start(step)
+
+    def y_wait(s, carry):
+        src = (yy + s) & 7
+        pltpu.make_async_remote_copy(
+            rot_hbm, ya.at[src], y_send.at[s], y_recv.at[src],
+            device_id=(za, src * 8 + xc), device_id_type=MESH).wait_recv()
+        return carry
+
+    lax.fori_loop(1, 8, y_wait, 0)
+    reads[1].wait()
+
+    def x_copy(s, slot):
+        peer = (xx + s) & 3
+        return pltpu.make_async_remote_copy(
+            ya, xb.at[pl.ds(8 * slot, 8)], x_send.at[s], x_recv.at[slot],
+            device_id=(za, yy * 8 + peer * 2 + cc), device_id_type=MESH)
+
+    for s in range(1, 4):
+        x_copy(s, xx).start()
+    for step in Y_ORDER[EARLY:]:
+        g_start(step)
+
+    for read in reads[:1] + reads[2:]:
         read.wait()
+    xb[pl.ds(8 * xx, 8)] = ya[...]
 
     lane3 = iota((3, 128), 1)
     for tile in range(16):
@@ -98,7 +162,6 @@
         lat[:, 128 * tile : 128 * tile + 128] = out
     third[...] = iota((8, 2048), 0) * lat[2:3, :]
     xg[...] = jnp.zeros_like(xg)
-    ya[yy] = rot[...]
 
     def phases(b, carry):
         first = (b >> 2) * lat[0:1, :]
@@ -112,70 +175,7 @@
         sinp[rows, :] = wave(t + 6).astype(BF16)
         return carry
 
-    pl.semaphore_wait(barrier, PB - 1 + KA - 1)
-
-    def y_copy(s):
-        peer = (yy + s) & 7
-        return pltpu.make_async_remote_copy(
-            rot, ya.at[yy], y_send.at[s], y_recv.at[yy],
-            device_id=(za, peer * 8 + xc), device_id_type=MESH)
-
-    def y_start(s, carry):
-        y_copy(s).start()
-        return carry
-
-    lax.fori_loop(1, 8, y_start, 0)
-
-    def g_columns(d):
-        return g.at[0, :, pl.ds(pl.multiple_of(worker_index(d) * COLS, COLS), COLS)]
-
-    @pl.when(working)
-    def _():
-        pltpu.make_async_copy(g_columns(me), recv1.at[me], g_recv.at[yy]).start()
-
-    def g_start(step):
-        base = ((yy + step) & 7) * 8
-
-        def one(u, carry):
-            d = base + (xc ^ u)
-
-            @pl.when(is_worker(d))
-            def _():
-                pltpu.make_async_remote_copy(
-                    g_columns(d), recv1.at[me], g_send.at[0], g_recv.at[yy],
-                    device_id=(za, d), device_id_type=MESH).start()
-
-            return carry
-
-        lax.fori_loop(0 if step else 1, 8, one, 0)
-
-    for step in Y_ORDER[:1]:
-        g_start(step)
-
-    lax.fori_loop(0, 8, phases, 0)
-
-    def y_wait(s, carry):
-        src = (yy + s) & 7
-        pltpu.make_async_remote_copy(
-            rot, ya.at[src], y_send.at[s], y_recv.at[src],
-            device_id=(za, src * 8 + xc), device_id_type=MESH).wait_recv()
-        return carry
-
-    lax.fori_loop(1, 8, y_wait, 0)
-
-    def x_copy(s, slot):
-        peer = (xx + s) & 3
-        return pltpu.make_async_remote_copy(
-            ya, xb.at[pl.ds(8 * slot, 8)], x_send.at[s], x_recv.at[slot],
-            device_id=(za, yy * 8 + peer * 2 + cc), device_id_type=MESH)
-
-    for s in range(1, 4):
-        x_copy(s, xx).start()
-    xb[pl.ds(8 * xx, 8)] = ya[...]
-
-    for step in Y_ORDER[1:3]:
-        g_start(step)
-    lax.fori_loop(8, 20, phases, 0)
+    lax.fori_loop(0, 32, phases, 0)
 
     for s in range(1, 4):
         x_copy(s, (xx + s) & 3).wait_recv()
@@ -191,10 +191,6 @@
 
     lax.fori_loop(1, KA, z_start, 0)
     zc[pl.ds((cc * 8 + za) * 32, 32)] = xb[...]
-
-    for step in Y_ORDER[3:]:
-        g_start(step)
-    lax.fori_loop(20, 32, phases, 0)
 
     def group(step):
         ys = (yy - step) & 7
@@ -207,14 +203,14 @@
         lanes = pl.ds(pl.multiple_of(ys * 256, 256), 256)
         total = jnp.dot(cosp[:, lanes], x, preferred_element_type=F32)
         total += jnp.dot(sinp[:, lanes], x_swapped, preferred_element_type=F32)
-        if step == 0:
+        if step == Y_ORDER[0]:
             acc[...] = total
         else:
             acc[...] += total
 
     @pl.when(working)
     def _():
-        for step in Y_ORDER[:5]:
+        for step in Y_ORDER[:MIDDLE]:
             group(step)
 
     def z_wait(s, carry):
@@ -232,7 +228,7 @@
 
     @pl.when(working)
     def _():
-        for step in Y_ORDER[5:]:
+        for step in Y_ORDER[MIDDLE:]:
             group(step)
         slot = worker_index(me)
 
@@ -420,7 +416,6 @@
         in_specs=[hbm] * 5,
         out_specs=(hbm, hbm, hbm),
         scratch_shapes=[
-            pltpu.VMEM((1, K), F32),
             pltpu.VMEM((1, K), jnp.int32),
             pltpu.SMEM((1, 8), jnp.int32),
             pltpu.VMEM((3, 1920), jnp.int32),

time: 56.9 us -> 52.4 us (0.921)
  Pallas kernels: 56.7 us -> 52.3 us
    pallas_call x1, Pallas kernels: 53.5 us -> 49 us  [per_device(): pl.pallas_call(comm_kernel, out_shape=(jax.ShapeDtypeStruct((WORKERS, 16,...]
where the time goes in v3:
time: 52.4 us; the launch traced here: 52.3 us
  Pallas kernels  52.3 us (100%)
    pallas_call x1, Pallas kernels, per_device(): pl.pallas_call(comm_kernel, out_shape=(jax.ShapeDtypeStruct((WORKERS, 16,...  49 us
    pallas_call x1, Pallas kernels, per_device(): pl.pallas_call(rotate_kernel, out_shape=jax.ShapeDtypeStruct((1, 8, NW *...  3.26 us

profile of v3, /device:TPU:1, one launch (start us, length us, event | category | flops | bytes accessed | tf_op | source)
XLA Modules:
  0.0 52.3 jit_solution(7731818084639915379)
XLA Ops:
  0.0 49.0 %exchange.1 = (bf16[54,16,128]{2,1,0:T(8,128)(2,1)}, bf16[256,256]{1,0:T(8,128)(2,1)}, bf16[256,256]{1,0:T(8,128)(2,1)}) custom-call(bf16[1,30,13824]{2,1,0:T(8,128)(2,1)} %g.1, f32[1,512]{1,0:T(1,128)} %rot_hbm.1, s32[1,512]{1,0:T(1,128)} %bitcast.1, s32[1,8]{1,0:T(1,128)} %shifted_hbm.1, s32[3,1920]{1,0:T(4,128)} %lattice_hbm.1), custom_call_target="tpu_custom_call" | custom-call | tf_op jit(solution)/shard_map/exchange/pallas_call | solution.py:409
  49.0 3.3 %rotate.1 = bf16[1,8,13824]{2,1,0:T(8,128)(2,1)} custom-call(bf16[54,16,128]{2,1,0:T(8,128)(2,1)} %get-tuple-element.8.blk_hbm, bf16[256,256]{1,0:T(8,128)(2,1)} %get-tuple-element.9.lhs1_hbm, bf16[256,256]{1,0:T(8,128)(2,1)} %get-tuple-element.10.lhs2_hbm, s32[1,8]{1,0:T(1,128)} %counts_hbm.1), custom_call_target="tpu_custom_call" | custom-call | tf_op jit(solution)/shard_map/rotate/pallas_call | solution.py:445

commit v4 on v3

--- a/solution.py
+++ b/solution.py
@@ -13,8 +13,9 @@
 PB = 64
 KA = 8
 Y_ORDER = (1, 7, 2, 6, 3, 5, 4, 0)
-EARLY = 4
-MIDDLE = 4
+B_ORDER = (4, 3, 5, 2, 6, 1, 7, 0)
+EARLY = 3
+MIDDLE = 6
 WORKERS = 54
 COLS = 256
 MESH = pl.DeviceIdType.MESH
@@ -50,8 +51,8 @@
 
 def comm_kernel(
     g, rot_hbm, home_hbm, shifted_hbm, lattice_hbm, blk_out, lhs1_out, lhs2_out,
-    home, shifted, lattice, recv1, xg, acc, cosp, sinp, send2, ya, xb, zc, lat, third, lh, ll, lhs1, lhs2,
-    in_sem, g_send, g_recv, b_send, b_recv, y_send, y_recv, x_send, x_recv, z_send, z_recv, c_send, c_recv, out_sem,
+    home, shifted, lattice, recv1, xg, acc, table, send2, ya, xb, zc, lat, third, lh, lhs1, lhs2,
+    in_sem, g_send, g_recv, b_send, b_recv, y_send, y_recv, x_send, x_recv, z_send, z_recv, c_send, c_recv, out_sem, above,
 ):
     za = lax.axis_index("ka")
     me = lax.axis_index("pb")
@@ -76,12 +77,12 @@
     lax.fori_loop(1, PB, greet, 0)
 
     def greet_z(s, carry):
-        pl.semaphore_signal(barrier, inc=1, device_id=(za ^ s, me), device_id_type=MESH)
-        return carry
-
-    lax.fori_loop(1, KA, greet_z, 0)
-
-    pl.semaphore_wait(barrier, PB - 1 + KA - 1)
+        pl.semaphore_signal(barrier, inc=1, device_id=(za + s, me), device_id_type=MESH)
+        return carry
+
+    lax.fori_loop(1, KA - za, greet_z, 0)
+
+    pl.semaphore_wait(barrier, PB - 1 + za)
 
     def y_copy(s):
         peer = (yy + s) & 7
@@ -131,10 +132,13 @@
     lax.fori_loop(1, 8, y_wait, 0)
     reads[1].wait()
 
+    line = jnp.concatenate([ya[y] for y in range(8)], axis=0)
+    xb[xx] = jnp.concatenate([line[:, :256], line[:, 256:]], axis=0).astype(BF16)
+
     def x_copy(s, slot):
         peer = (xx + s) & 3
         return pltpu.make_async_remote_copy(
-            ya, xb.at[pl.ds(8 * slot, 8)], x_send.at[s], x_recv.at[slot],
+            xb.at[xx], xb.at[slot], x_send.at[s], x_recv.at[slot],
             device_id=(za, yy * 8 + peer * 2 + cc), device_id_type=MESH)
 
     for s in range(1, 4):
@@ -142,9 +146,14 @@
     for step in Y_ORDER[EARLY:]:
         g_start(step)
 
+    def greet_lower(s, carry):
+        pl.semaphore_signal(above, inc=1, device_id=(za - s, me), device_id_type=MESH)
+        return carry
+
+    lax.fori_loop(1, za + 1, greet_lower, 0)
+
     for read in reads[:1] + reads[2:]:
         read.wait()
-    xb[pl.ds(8 * xx, 8)] = ya[...]
 
     lane3 = iota((3, 128), 1)
     for tile in range(16):
@@ -171,8 +180,12 @@
         high = (first + (k2 + 1) * second) + third[...]
         t = jnp.concatenate([low, high], axis=0)
         rows = pl.ds(pl.multiple_of(b * 16, 16), 16)
-        cosp[rows, :] = wave(t).astype(BF16)
-        sinp[rows, :] = wave(t + 6).astype(BF16)
+        cosines = wave(t).astype(BF16)
+        sines = wave(t + 6).astype(BF16)
+        for ys in range(8):
+            lanes = slice(256 * ys, 256 * ys + 256)
+            table[rows, 512 * ys : 512 * ys + 256] = cosines[:, lanes]
+            table[rows, 512 * ys + 256 : 512 * ys + 512] = sines[:, lanes]
         return carry
 
     lax.fori_loop(0, 32, phases, 0)
@@ -182,15 +195,19 @@
 
     def z_copy(s, slot):
         return pltpu.make_async_remote_copy(
-            xb, zc.at[pl.ds((cc * 8 + slot) * 32, 32)], z_send.at[s], z_recv.at[slot],
+            xb, zc.at[pl.ds((cc * 8 + slot) * 4, 4)], z_send.at[s], z_recv.at[slot],
             device_id=((za + s) & 7, me), device_id_type=MESH)
 
     def z_start(s, carry):
         z_copy(s, za).start()
         return carry
 
+    @pl.when(za < KA - 1)
+    def _():
+        pl.semaphore_wait(above, KA - 1 - za)
+
     lax.fori_loop(1, KA, z_start, 0)
-    zc[pl.ds((cc * 8 + za) * 32, 32)] = xb[...]
+    zc[pl.ds((cc * 8 + za) * 4, 4)] = xb[...]
 
     def group(step):
         ys = (yy - step) & 7
@@ -200,9 +217,9 @@
             xg[u, 0:ROWS, :] = recv1[ys * 8 + u]
         x = xg[...].reshape(256, COLS)
         x_swapped = swap_parts(x.astype(F32)).astype(BF16)
-        lanes = pl.ds(pl.multiple_of(ys * 256, 256), 256)
-        total = jnp.dot(cosp[:, lanes], x, preferred_element_type=F32)
-        total += jnp.dot(sinp[:, lanes], x_swapped, preferred_element_type=F32)
+        lanes = pl.ds(pl.multiple_of(ys * 512, 512), 512)
+        total = jnp.dot(
+            table[:, lanes], jnp.concatenate([x, x_swapped], axis=0), preferred_element_type=F32)
         if step == Y_ORDER[0]:
             acc[...] = total
         else:
@@ -220,7 +237,7 @@
     lax.fori_loop(1, KA, z_wait, 0)
 
     def c_copy(half):
-        part = zc.at[pl.ds(half * 256, 256)]
+        part = zc.at[pl.ds(half * 32, 32)]
         return pltpu.make_async_remote_copy(
             part, part, c_send.at[0], c_recv.at[0], device_id=(za, me ^ 1), device_id_type=MESH)
 
@@ -232,55 +249,61 @@
             group(step)
         slot = worker_index(me)
 
-        def pack(s, carry):
-            d = me ^ s
-            rows = acc[pl.ds(pl.multiple_of(8 * d, 8), 8), :]
-            send2[d] = jnp.concatenate([rows[:, :128], rows[:, 128:]], axis=0).astype(BF16)
-
-            @pl.when(s > 0)
-            def _():
+        for step in B_ORDER:
+            base = ((yy + step) & 7) * 8
+            rows = acc[pl.ds(pl.multiple_of(base * 8, 64), 64), :]
+            for u in range(8):
+                part = rows[8 * u : 8 * u + 8]
+                send2[base + u] = jnp.concatenate([part[:, :128], part[:, 128:]], axis=0).astype(BF16)
+
+            def one(u, carry):
+                d = base + (xc ^ u)
                 pltpu.make_async_remote_copy(
                     send2.at[d], blk_out.at[slot], b_send.at[0], b_recv.at[0],
                     device_id=(za, d), device_id_type=MESH).start()
-
-            return carry
-
-        lax.fori_loop(0, PB, pack, 0)
+                return carry
+
+            lax.fori_loop(0 if step else 1, 8, one, 0)
         pltpu.make_async_copy(send2.at[me], blk_out.at[slot], b_recv.at[0]).start()
 
     c_copy(1 - cc).wait_recv()
     r = iota((1, K), 1)
     place = (((r & 1) * 8 + (r >> 6)) * 4 + ((r >> 1) & 3)) * 8 + ((r >> 3) & 7)
     sub = iota((8, K), 0)
+    sub8 = iota((8, 256), 0)
+
+    def pick(point):
+        at = jnp.minimum(jnp.sum(jnp.where(home[...] == point, place, 0)), K - 1)
+        block = zc[at >> 3].astype(F32)
+        here = sub8 == (at & 7)
+        halves = [
+            jnp.sum(jnp.where(here, block[8 * h : 8 * h + 8], 0.0), axis=0, keepdims=True) for h in range(2)
+        ]
+        return jnp.concatenate(halves, axis=1)
+
     own = jnp.zeros((8, K), F32)
     other = jnp.zeros((8, K), F32)
     for k in range(8):
-        at = jnp.minimum(jnp.sum(jnp.where(home[...] == me * 8 + k, place, 0)), K - 1)
-        own = jnp.where(sub == k, zc[at], own)
-        at = jnp.minimum(jnp.sum(jnp.where(home[...] == shifted[0, k], place, 0)), K - 1)
-        other = jnp.where(sub == k, zc[at], other)
+        own = jnp.where(sub == k, pick(me * 8 + k), own)
+        other = jnp.where(sub == k, pick(shifted[0, k]), other)
     both = jnp.concatenate([own, other], axis=0)
     for jp in range(32):
         pieces = [both[:, 128 * v : 128 * v + 128] for v in range(4)]
         if jp:
             pieces = [pltpu.roll(piece, 128 - jp, axis=1) for piece in pieces]
-        turned = jnp.concatenate(pieces, axis=1)
-        upper = turned.astype(BF16)
-        lh[16 * jp : 16 * jp + 16, :] = upper
-        ll[16 * jp : 16 * jp + 16, :] = (turned - upper.astype(F32)).astype(BF16)
+        lh[16 * jp : 16 * jp + 16, :] = jnp.concatenate(pieces, axis=1).astype(BF16)
     spread = jnp.where(iota((K, 128), 0) == 32 * (iota((K, 128), 1) // 8), 1.0, 0.0).astype(BF16)
     keep = iota((K, 128), 1) % 8 == iota((K, 128), 0) % 8
-    for level, source in ((0, lh), (1, ll)):
-        full = jnp.where(keep, jnp.dot(source[...], spread, preferred_element_type=F32), 0.0)
-        for jj in range(8):
-            for part in range(2):
-                a = 16 * (4 * jj + part)
-                b = 16 * (4 * jj + 2 + part)
-                rows = slice(128 * level + 16 * jj, 128 * level + 16 * jj + 16)
-                lanes = slice(128 * part, 128 * part + 128)
-                lhs1[rows, lanes] = jnp.concatenate([full[a : a + 8], full[b : b + 8]], axis=0).astype(BF16)
-                left = jnp.concatenate([full[a + 8 : a + 16], full[b + 8 : b + 16]], axis=0)
-                lhs2[rows, lanes] = (left if part == 0 else -left).astype(BF16)
+    full = jnp.where(keep, jnp.dot(lh[...], spread, preferred_element_type=F32), 0.0)
+    for jj in range(8):
+        for part in range(2):
+            a = 16 * (4 * jj + part)
+            b = 16 * (4 * jj + 2 + part)
+            rows = slice(16 * jj, 16 * jj + 16)
+            lanes = slice(128 * part, 128 * part + 128)
+            lhs1[rows, lanes] = jnp.concatenate([full[a : a + 8], full[b : b + 8]], axis=0).astype(BF16)
+            left = jnp.concatenate([full[a + 8 : a + 16], full[b + 8 : b + 16]], axis=0)
+            lhs2[rows, lanes] = (left if part == 0 else -left).astype(BF16)
     outs = [pltpu.make_async_copy(lhs1, lhs1_out, out_sem.at[0]), pltpu.make_async_copy(lhs2, lhs2_out, out_sem.at[1])]
     for out in outs:
         out.start()
@@ -358,8 +381,7 @@
         lanes = slice(256 * p, 256 * p + 256)
         x = padded[:, lanes]
         rhs = jnp.concatenate([x, swap_parts(x)], axis=0).astype(BF16)
-        both = jnp.dot(lhs1[...], rhs, preferred_element_type=F32)
-        middle[:, lanes] = both[:128] + both[128:]
+        middle[:, lanes] = jnp.dot(lhs1[...], rhs, preferred_element_type=F32)
 
     for a in range(8):
         for b in range(8):
@@ -384,8 +406,8 @@
         x = jnp.concatenate([x, swap_parts(x)], axis=0)
         upper = x.astype(BF16)
         lower = (x - upper.astype(F32)).astype(BF16)
-        both = jnp.dot(lhs2[...], upper, preferred_element_type=F32)
-        total = both[:128] + (both[128:] + jnp.dot(lhs2[:128, :], lower, preferred_element_type=F32))
+        total = jnp.dot(lhs2[...], upper, preferred_element_type=F32)
+        total += jnp.dot(lhs2[...], lower, preferred_element_type=F32)
         band = jnp.maximum(row // 8, 4 * p + iota((128, 256), 1) // 64)
         final[:, lanes] = jnp.where(band < limits, total, 0.0)
 
@@ -410,8 +432,8 @@
         comm_kernel,
         out_shape=(
             jax.ShapeDtypeStruct((WORKERS, 16, 128), BF16),
-            jax.ShapeDtypeStruct((256, 256), BF16),
-            jax.ShapeDtypeStruct((256, 256), BF16),
+            jax.ShapeDtypeStruct((128, 256), BF16),
+            jax.ShapeDtypeStruct((128, 256), BF16),
         ),
         in_specs=[hbm] * 5,
         out_specs=(hbm, hbm, hbm),
@@ -422,20 +444,19 @@
             pltpu.VMEM((PB, ROWS, COLS), BF16),
             pltpu.VMEM((8, 32, COLS), BF16),
             pltpu.VMEM((K, COLS), F32),
-            pltpu.VMEM((K, 2048), BF16),
-            pltpu.VMEM((K, 2048), BF16),
+            pltpu.VMEM((K, 4096), BF16),
             pltpu.VMEM((PB, 16, 128), BF16),
             pltpu.VMEM((8, 1, 512), F32),
-            pltpu.VMEM((32, 1, 512), F32),
-            pltpu.VMEM((512, 1, 512), F32),
+            pltpu.VMEM((4, 16, 256), BF16),
+            pltpu.VMEM((64, 16, 256), BF16),
             pltpu.VMEM((3, 2048), jnp.int32),
             pltpu.VMEM((8, 2048), jnp.int32),
             pltpu.VMEM((K, 512), BF16),
-            pltpu.VMEM((K, 512), BF16),
-            pltpu.VMEM((256, 256), BF16),
-            pltpu.VMEM((256, 256), BF16),
+            pltpu.VMEM((128, 256), BF16),
+            pltpu.VMEM((128, 256), BF16),
             dma((4,)), dma((1,)), dma((8,)), dma((1,)), dma((1,)),
             dma((8,)), dma((8,)), dma((4,)), dma((4,)), dma((8,)), dma((8,)), dma((1,)), dma((1,)), dma((2,)),
+            pltpu.SemaphoreType.REGULAR,
         ],
         compiler_params=pltpu.CompilerParams(
             collective_id=0, has_side_effects=True, vmem_limit_bytes=60 * 1024 * 1024
@@ -449,8 +470,8 @@
         out_specs=vmem,
         scratch_shapes=[
             pltpu.VMEM((WORKERS, 16, 128), BF16),
-            pltpu.VMEM((256, 256), BF16),
-            pltpu.VMEM((256, 256), BF16),
+            pltpu.VMEM((128, 256), BF16),
+            pltpu.VMEM((128, 256), BF16),
             pltpu.SMEM((1, 8), jnp.int32),
             pltpu.VMEM((128, 1024), F32),
             pltpu.VMEM((128, 1024), F32),

time: 52.4 us -> 49 us (0.935)
  Pallas kernels: 52.3 us -> 48.9 us
    pallas_call x1, Pallas kernels: 49 us -> 45.6 us  [per_device(): pl.pallas_call(comm_kernel, out_shape=(jax.ShapeDtypeStruct((WORKERS, 16,...]
where the time goes in v4:
time: 49 us; the launch traced here: 48.9 us
  Pallas kernels  48.9 us (100%)
    pallas_call x1, Pallas kernels, per_device(): pl.pallas_call(comm_kernel, out_shape=(jax.ShapeDtypeStruct((WORKERS, 16,...  45.6 us
    pallas_call x1, Pallas kernels, per_device(): pl.pallas_call(rotate_kernel, out_shape=jax.ShapeDtypeStruct((1, 8, NW *...  3.27 us

profile of v4, /device:TPU:1, one launch (start us, length us, event | category | flops | bytes accessed | tf_op | source)
XLA Modules:
  0.0 48.9 jit_solution(7199195478400086746)
XLA Ops:
  0.0 45.6 %exchange.1 = (bf16[54,16,128]{2,1,0:T(8,128)(2,1)}, bf16[128,256]{1,0:T(8,128)(2,1)}, bf16[128,256]{1,0:T(8,128)(2,1)}) custom-call(bf16[1,30,13824]{2,1,0:T(8,128)(2,1)} %g.1, f32[1,512]{1,0:T(1,128)} %rot_hbm.1, s32[1,512]{1,0:T(1,128)} %bitcast.1, s32[1,8]{1,0:T(1,128)} %shifted_hbm.1, s32[3,1920]{1,0:T(4,128)} %lattice_hbm.1), custom_call_target="tpu_custom_call" | custom-call | tf_op jit(solution)/shard_map/exchange/pallas_call | solution.py:431
  45.6 3.3 %rotate.1 = bf16[1,8,13824]{2,1,0:T(8,128)(2,1)} custom-call(bf16[54,16,128]{2,1,0:T(8,128)(2,1)} %get-tuple-element.8.blk_hbm, bf16[128,256]{1,0:T(8,128)(2,1)} %get-tuple-element.9.lhs1_hbm, bf16[128,256]{1,0:T(8,128)(2,1)} %get-tuple-element.10.lhs2_hbm, s32[1,8]{1,0:T(1,128)} %counts_hbm.1), custom_call_target="tpu_custom_call" | custom-call | tf_op jit(solution)/shard_map/rotate/pallas_call | solution.py:466

commit v5 on v4

--- a/solution.py
+++ b/solution.py
@@ -14,8 +14,8 @@
 KA = 8
 Y_ORDER = (1, 7, 2, 6, 3, 5, 4, 0)
 B_ORDER = (4, 3, 5, 2, 6, 1, 7, 0)
-EARLY = 3
-MIDDLE = 6
+EARLY = 4
+MIDDLE = 8
 WORKERS = 54
 COLS = 256
 MESH = pl.DeviceIdType.MESH
@@ -51,7 +51,7 @@
 
 def comm_kernel(
     g, rot_hbm, home_hbm, shifted_hbm, lattice_hbm, blk_out, lhs1_out, lhs2_out,
-    home, shifted, lattice, recv1, xg, acc, table, send2, ya, xb, zc, lat, third, lh, lhs1, lhs2,
+    gv, home, shifted, lattice, recv1, xg, acc, table, send2, ya, xb, zc, lat, third, lh, lhs1, lhs2,
     in_sem, g_send, g_recv, b_send, b_recv, y_send, y_recv, x_send, x_recv, z_send, z_recv, c_send, c_recv, out_sem, above,
 ):
     za = lax.axis_index("ka")
@@ -67,6 +67,8 @@
         for i, (source, target) in enumerate(
             ((lattice_hbm, lattice), (rot_hbm, ya.at[yy]), (home_hbm, home), (shifted_hbm, shifted)))
     ]
+    fetch = pltpu.make_async_copy(g.at[0], gv, in_sem.at[4])
+    fetch.start()
     for read in reads:
         read.start()
 
@@ -82,6 +84,7 @@
 
     lax.fori_loop(1, KA - za, greet_z, 0)
 
+    fetch.wait()
     pl.semaphore_wait(barrier, PB - 1 + za)
 
     def y_copy(s):
@@ -97,7 +100,7 @@
     lax.fori_loop(1, 8, y_start, 0)
 
     def g_columns(d):
-        return g.at[0, :, pl.ds(pl.multiple_of(worker_index(d) * COLS, COLS), COLS)]
+        return gv.at[:, pl.ds(pl.multiple_of(worker_index(d) * COLS, COLS), COLS)]
 
     @pl.when(working)
     def _():
@@ -438,6 +441,7 @@
         in_specs=[hbm] * 5,
         out_specs=(hbm, hbm, hbm),
         scratch_shapes=[
+            pltpu.VMEM((ROWS, NW * NW * VEC), BF16),
             pltpu.VMEM((1, K), jnp.int32),
             pltpu.SMEM((1, 8), jnp.int32),
             pltpu.VMEM((3, 1920), jnp.int32),
@@ -454,7 +458,7 @@
             pltpu.VMEM((K, 512), BF16),
             pltpu.VMEM((128, 256), BF16),
             pltpu.VMEM((128, 256), BF16),
-            dma((4,)), dma((1,)), dma((8,)), dma((1,)), dma((1,)),
+            dma((5,)), dma((1,)), dma((8,)), dma((1,)), dma((1,)),
             dma((8,)), dma((8,)), dma((4,)), dma((4,)), dma((8,)), dma((8,)), dma((1,)), dma((1,)), dma((2,)),
             pltpu.SemaphoreType.REGULAR,
         ],

time: 49 us -> 48 us (0.980)
  Pallas kernels: 48.9 us -> 47.8 us
    pallas_call x1, Pallas kernels: 45.6 us -> 44.5 us  [per_device(): pl.pallas_call(comm_kernel, out_shape=(jax.ShapeDtypeStruct((WORKERS, 16,...]
where the time goes in v5:
time: 48 us; the launch traced here: 47.8 us
  Pallas kernels  47.8 us (100%)
    pallas_call x1, Pallas kernels, per_device(): pl.pallas_call(comm_kernel, out_shape=(jax.ShapeDtypeStruct((WORKERS, 16,...  44.5 us
    pallas_call x1, Pallas kernels, per_device(): pl.pallas_call(rotate_kernel, out_shape=jax.ShapeDtypeStruct((1, 8, NW *...  3.28 us

profile of v5, /device:TPU:1, one launch (start us, length us, event | category | flops | bytes accessed | tf_op | source)
XLA Modules:
  0.0 47.8 jit_solution(2205548368705347888)
XLA Ops:
  0.0 44.5 %exchange.1 = (bf16[54,16,128]{2,1,0:T(8,128)(2,1)}, bf16[128,256]{1,0:T(8,128)(2,1)}, bf16[128,256]{1,0:T(8,128)(2,1)}) custom-call(bf16[1,30,13824]{2,1,0:T(8,128)(2,1)} %g.1, f32[1,512]{1,0:T(1,128)} %rot_hbm.1, s32[1,512]{1,0:T(1,128)} %bitcast.1, s32[1,8]{1,0:T(1,128)} %shifted_hbm.1, s32[3,1920]{1,0:T(4,128)} %lattice_hbm.1), custom_call_target="tpu_custom_call" | custom-call | tf_op jit(solution)/shard_map/exchange/pallas_call | solution.py:434
  44.6 3.3 %rotate.1 = bf16[1,8,13824]{2,1,0:T(8,128)(2,1)} custom-call(bf16[54,16,128]{2,1,0:T(8,128)(2,1)} %get-tuple-element.8.blk_hbm, bf16[128,256]{1,0:T(8,128)(2,1)} %get-tuple-element.9.lhs1_hbm, bf16[128,256]{1,0:T(8,128)(2,1)} %get-tuple-element.10.lhs2_hbm, s32[1,8]{1,0:T(1,128)} %counts_hbm.1), custom_call_target="tpu_custom_call" | custom-call | tf_op jit(solution)/shard_map/rotate/pallas_call | solution.py:470

commit v6 on v5

--- a/solution.py
+++ b/solution.py
@@ -12,10 +12,9 @@
 ROWS = 30
 PB = 64
 KA = 8
-Y_ORDER = (1, 7, 2, 6, 3, 5, 4, 0)
+Y_ORDER = (2, 6, 3, 5, 1, 7, 4, 0)
 B_ORDER = (4, 3, 5, 2, 6, 1, 7, 0)
 EARLY = 4
-MIDDLE = 8
 WORKERS = 54
 COLS = 256
 MESH = pl.DeviceIdType.MESH
@@ -51,7 +50,7 @@
 
 def comm_kernel(
     g, rot_hbm, home_hbm, shifted_hbm, lattice_hbm, blk_out, lhs1_out, lhs2_out,
-    gv, home, shifted, lattice, recv1, xg, acc, table, send2, ya, xb, zc, lat, third, lh, lhs1, lhs2,
+    gv, home, shifted, lattice, recv1, xg, acc, table, send2, ya, xb, zc, lat, third, lh, lhs1, lhs2, mate, give, take,
     in_sem, g_send, g_recv, b_send, b_recv, y_send, y_recv, x_send, x_recv, z_send, z_recv, c_send, c_recv, out_sem, above,
 ):
     za = lax.axis_index("ka")
@@ -99,6 +98,12 @@
 
     lax.fori_loop(1, 8, y_start, 0)
 
+    def mate_copy():
+        return pltpu.make_async_remote_copy(
+            shifted_hbm, mate, c_send.at[1], c_recv.at[1], device_id=(za, me ^ 1), device_id_type=MESH)
+
+    mate_copy().start()
+
     def g_columns(d):
         return gv.at[:, pl.ds(pl.multiple_of(worker_index(d) * COLS, COLS), COLS)]
 
@@ -198,7 +203,7 @@
 
     def z_copy(s, slot):
         return pltpu.make_async_remote_copy(
-            xb, zc.at[pl.ds((cc * 8 + slot) * 4, 4)], z_send.at[s], z_recv.at[slot],
+            xb, zc.at[pl.ds(slot * 4, 4)], z_send.at[s], z_recv.at[slot],
             device_id=((za + s) & 7, me), device_id_type=MESH)
 
     def z_start(s, carry):
@@ -210,7 +215,7 @@
         pl.semaphore_wait(above, KA - 1 - za)
 
     lax.fori_loop(1, KA, z_start, 0)
-    zc[pl.ds((cc * 8 + za) * 4, 4)] = xb[...]
+    zc[pl.ds(za * 4, 4)] = xb[...]
 
     def group(step):
         ys = (yy - step) & 7
@@ -230,25 +235,7 @@
 
     @pl.when(working)
     def _():
-        for step in Y_ORDER[:MIDDLE]:
-            group(step)
-
-    def z_wait(s, carry):
-        z_copy(s, (za + s) & 7).wait_recv()
-        return carry
-
-    lax.fori_loop(1, KA, z_wait, 0)
-
-    def c_copy(half):
-        part = zc.at[pl.ds(half * 32, 32)]
-        return pltpu.make_async_remote_copy(
-            part, part, c_send.at[0], c_recv.at[0], device_id=(za, me ^ 1), device_id_type=MESH)
-
-    c_copy(cc).start()
-
-    @pl.when(working)
-    def _():
-        for step in Y_ORDER[MIDDLE:]:
+        for step in Y_ORDER:
             group(step)
         slot = worker_index(me)
 
@@ -269,7 +256,12 @@
             lax.fori_loop(0 if step else 1, 8, one, 0)
         pltpu.make_async_copy(send2.at[me], blk_out.at[slot], b_recv.at[0]).start()
 
-    c_copy(1 - cc).wait_recv()
+    def z_wait(s, carry):
+        z_copy(s, (za + s) & 7).wait_recv()
+        return carry
+
+    lax.fori_loop(1, KA, z_wait, 0)
+    mate_copy().wait_recv()
     r = iota((1, K), 1)
     place = (((r & 1) * 8 + (r >> 6)) * 4 + ((r >> 1) & 3)) * 8 + ((r >> 3) & 7)
     sub = iota((8, K), 0)
@@ -277,19 +269,31 @@
 
     def pick(point):
         at = jnp.minimum(jnp.sum(jnp.where(home[...] == point, place, 0)), K - 1)
-        block = zc[at >> 3].astype(F32)
-        here = sub8 == (at & 7)
+        block = zc[(at >> 3) & 31].astype(F32)
+        here = sub8 == (at & 7) + 8 * ((at >> 8) ^ cc)
         halves = [
             jnp.sum(jnp.where(here, block[8 * h : 8 * h + 8], 0.0), axis=0, keepdims=True) for h in range(2)
         ]
         return jnp.concatenate(halves, axis=1)
 
-    own = jnp.zeros((8, K), F32)
-    other = jnp.zeros((8, K), F32)
-    for k in range(8):
-        own = jnp.where(sub == k, pick(me * 8 + k), own)
-        other = jnp.where(sub == k, pick(shifted[0, k]), other)
-    both = jnp.concatenate([own, other], axis=0)
+    def picked(first, moved):
+        own = jnp.zeros((8, K), F32)
+        other = jnp.zeros((8, K), F32)
+        for k in range(8):
+            own = jnp.where(sub == k, pick(first + k), own)
+            other = jnp.where(sub == k, pick(moved[:, k : k + 1]), other)
+        return jnp.concatenate([own, other], axis=0)
+
+    give[...] = picked((me ^ 1) * 8, mate[...])
+
+    def c_copy():
+        return pltpu.make_async_remote_copy(
+            give, take, c_send.at[0], c_recv.at[0], device_id=(za, me ^ 1), device_id_type=MESH)
+
+    c_copy().start()
+    both = picked(me * 8, shifted[...])
+    c_copy().wait_recv()
+    both += take[...]
     for jp in range(32):
         pieces = [both[:, 128 * v : 128 * v + 128] for v in range(4)]
         if jp:
@@ -324,7 +328,8 @@
         return carry
 
     lax.fori_loop(1, KA, z_left, 0)
-    c_copy(cc).wait_send()
+    c_copy().wait_send()
+    mate_copy().wait_send()
 
     @pl.when(working)
     def _():
@@ -443,7 +448,7 @@
         scratch_shapes=[
             pltpu.VMEM((ROWS, NW * NW * VEC), BF16),
             pltpu.VMEM((1, K), jnp.int32),
-            pltpu.SMEM((1, 8), jnp.int32),
+            pltpu.VMEM((1, 8), jnp.int32),
             pltpu.VMEM((3, 1920), jnp.int32),
             pltpu.VMEM((PB, ROWS, COLS), BF16),
             pltpu.VMEM((8, 32, COLS), BF16),
@@ -452,14 +457,17 @@
             pltpu.VMEM((PB, 16, 128), BF16),
             pltpu.VMEM((8, 1, 512), F32),
             pltpu.VMEM((4, 16, 256), BF16),
-            pltpu.VMEM((64, 16, 256), BF16),
+            pltpu.VMEM((32, 16, 256), BF16),
             pltpu.VMEM((3, 2048), jnp.int32),
             pltpu.VMEM((8, 2048), jnp.int32),
             pltpu.VMEM((K, 512), BF16),
             pltpu.VMEM((128, 256), BF16),
             pltpu.VMEM((128, 256), BF16),
+            pltpu.VMEM((1, 8), jnp.int32),
+            pltpu.VMEM((16, K), F32),
+            pltpu.VMEM((16, K), F32),
             dma((5,)), dma((1,)), dma((8,)), dma((1,)), dma((1,)),
-            dma((8,)), dma((8,)), dma((4,)), dma((4,)), dma((8,)), dma((8,)), dma((1,)), dma((1,)), dma((2,)),
+            dma((8,)), dma((8,)), dma((4,)), dma((4,)), dma((8,)), dma((8,)), dma((2,)), dma((2,)), dma((2,)),
             pltpu.SemaphoreType.REGULAR,
         ],
         compiler_params=pltpu.CompilerParams(

time: 48 us -> 47.1 us (0.981)
  Pallas kernels: 47.8 us -> 47 us
    pallas_call x1, Pallas kernels: 44.5 us -> 43.7 us  [per_device(): pl.pallas_call(comm_kernel, out_shape=(jax.ShapeDtypeStruct((WORKERS, 16,...]
where the time goes in v6:
time: 47.1 us; the launch traced here: 47 us
  Pallas kernels  47 us (100%)
    pallas_call x1, Pallas kernels, per_device(): pl.pallas_call(comm_kernel, out_shape=(jax.ShapeDtypeStruct((WORKERS, 16,...  43.7 us
    pallas_call x1, Pallas kernels, per_device(): pl.pallas_call(rotate_kernel, out_shape=jax.ShapeDtypeStruct((1, 8, NW *...  3.28 us

profile of v6, /device:TPU:1, one launch (start us, length us, event | category | flops | bytes accessed | tf_op | source)
XLA Modules:
  0.0 47.0 jit_solution(9782232482417676370)
XLA Ops:
  0.0 43.7 %exchange.1 = (bf16[54,16,128]{2,1,0:T(8,128)(2,1)}, bf16[128,256]{1,0:T(8,128)(2,1)}, bf16[128,256]{1,0:T(8,128)(2,1)}) custom-call(bf16[1,30,13824]{2,1,0:T(8,128)(2,1)} %g.1, f32[1,512]{1,0:T(1,128)} %rot_hbm.1, s32[1,512]{1,0:T(1,128)} %bitcast.1, s32[1,8]{1,0:T(1,128)} %shifted_hbm.1, s32[3,1920]{1,0:T(4,128)} %lattice_hbm.1), custom_call_target="tpu_custom_call" | custom-call | tf_op jit(solution)/shard_map/exchange/pallas_call | solution.py:439
  43.7 3.3 %rotate.1 = bf16[1,8,13824]{2,1,0:T(8,128)(2,1)} custom-call(bf16[54,16,128]{2,1,0:T(8,128)(2,1)} %get-tuple-element.8.blk_hbm, bf16[128,256]{1,0:T(8,128)(2,1)} %get-tuple-element.9.lhs1_hbm, bf16[128,256]{1,0:T(8,128)(2,1)} %get-tuple-element.10.lhs2_hbm, s32[1,8]{1,0:T(1,128)} %counts_hbm.1), custom_call_target="tpu_custom_call" | custom-call | tf_op jit(solution)/shard_map/rotate/pallas_call | solution.py:478

commit v7 on v6

--- a/solution.py
+++ b/solution.py
@@ -247,13 +247,17 @@
                 send2[base + u] = jnp.concatenate([part[:, :128], part[:, 128:]], axis=0).astype(BF16)
 
             def one(u, carry):
-                d = base + (xc ^ u)
+                d = base + (xc ^ (u ^ 4))
                 pltpu.make_async_remote_copy(
                     send2.at[d], blk_out.at[slot], b_send.at[0], b_recv.at[0],
                     device_id=(za, d), device_id_type=MESH).start()
                 return carry
 
-            lax.fori_loop(0 if step else 1, 8, one, 0)
+            if step:
+                lax.fori_loop(0, 8, one, 0)
+            else:
+                lax.fori_loop(0, 4, one, 0)
+                lax.fori_loop(5, 8, one, 0)
         pltpu.make_async_copy(send2.at[me], blk_out.at[slot], b_recv.at[0]).start()
 
     def z_wait(s, carry):

time: 47.1 us -> 46.6 us (0.989)
  Pallas kernels: 47 us -> 46.3 us
    pallas_call x1, Pallas kernels: 43.7 us -> 43 us  [per_device(): pl.pallas_call(comm_kernel, out_shape=(jax.ShapeDtypeStruct((WORKERS, 16,...]
where the time goes in v7:
time: 46.6 us; the launch traced here: 46.3 us
  Pallas kernels  46.3 us (99%)
    pallas_call x1, Pallas kernels, per_device(): pl.pallas_call(comm_kernel, out_shape=(jax.ShapeDtypeStruct((WORKERS, 16,...  43 us
    pallas_call x1, Pallas kernels, per_device(): pl.pallas_call(rotate_kernel, out_shape=jax.ShapeDtypeStruct((1, 8, NW *...  3.28 us

profile of v7, /device:TPU:1, one launch (start us, length us, event | category | flops | bytes accessed | tf_op | source)
XLA Modules:
  0.0 46.3 jit_solution(6628520318434387614)
XLA Ops:
  0.0 43.0 %exchange.1 = (bf16[54,16,128]{2,1,0:T(8,128)(2,1)}, bf16[128,256]{1,0:T(8,128)(2,1)}, bf16[128,256]{1,0:T(8,128)(2,1)}) custom-call(bf16[1,30,13824]{2,1,0:T(8,128)(2,1)} %g.1, f32[1,512]{1,0:T(1,128)} %rot_hbm.1, s32[1,512]{1,0:T(1,128)} %bitcast.1, s32[1,8]{1,0:T(1,128)} %shifted_hbm.1, s32[3,1920]{1,0:T(4,128)} %lattice_hbm.1), custom_call_target="tpu_custom_call" | custom-call | tf_op jit(solution)/shard_map/exchange/pallas_call | solution.py:443
  43.0 3.3 %rotate.1 = bf16[1,8,13824]{2,1,0:T(8,128)(2,1)} custom-call(bf16[54,16,128]{2,1,0:T(8,128)(2,1)} %get-tuple-element.8.blk_hbm, bf16[128,256]{1,0:T(8,128)(2,1)} %get-tuple-element.9.lhs1_hbm, bf16[128,256]{1,0:T(8,128)(2,1)} %get-tuple-element.10.lhs2_hbm, s32[1,8]{1,0:T(1,128)} %counts_hbm.1), custom_call_target="tpu_custom_call" | custom-call | tf_op jit(solution)/shard_map/rotate/pallas_call | solution.py:482

commit v8 on v7

--- a/solution.py
+++ b/solution.py
@@ -247,7 +247,7 @@
                 send2[base + u] = jnp.concatenate([part[:, :128], part[:, 128:]], axis=0).astype(BF16)
 
             def one(u, carry):
-                d = base + (xc ^ (u ^ 4))
+                d = base + (xc ^ (u ^ (4 + 2 * (u >> 2))))
                 pltpu.make_async_remote_copy(
                     send2.at[d], blk_out.at[slot], b_send.at[0], b_recv.at[0],
                     device_id=(za, d), device_id_type=MESH).start()
@@ -256,8 +256,8 @@
             if step:
                 lax.fori_loop(0, 8, one, 0)
             else:
-                lax.fori_loop(0, 4, one, 0)
-                lax.fori_loop(5, 8, one, 0)
+                lax.fori_loop(0, 6, one, 0)
+                lax.fori_loop(7, 8, one, 0)
         pltpu.make_async_copy(send2.at[me], blk_out.at[slot], b_recv.at[0]).start()
 
     def z_wait(s, carry):

time: 46.6 us -> 46.4 us (level)
  no operation moved by 1% of the time
where the time goes in v8:
time: 46.4 us; the launch traced here: 46.2 us
  Pallas kernels  46.2 us (100%)
    pallas_call x1, Pallas kernels, per_device(): pl.pallas_call(comm_kernel, out_shape=(jax.ShapeDtypeStruct((WORKERS, 16,...  43 us
    pallas_call x1, Pallas kernels, per_device(): pl.pallas_call(rotate_kernel, out_shape=jax.ShapeDtypeStruct((1, 8, NW *...  3.28 us

profile of v8, /device:TPU:1, one launch (start us, length us, event | category | flops | bytes accessed | tf_op | source)
XLA Modules:
  0.0 46.2 jit_solution(11720658448416381638)
XLA Ops:
  0.0 43.0 %exchange.1 = (bf16[54,16,128]{2,1,0:T(8,128)(2,1)}, bf16[128,256]{1,0:T(8,128)(2,1)}, bf16[128,256]{1,0:T(8,128)(2,1)}) custom-call(bf16[1,30,13824]{2,1,0:T(8,128)(2,1)} %g.1, f32[1,512]{1,0:T(1,128)} %rot_hbm.1, s32[1,512]{1,0:T(1,128)} %bitcast.1, s32[1,8]{1,0:T(1,128)} %shifted_hbm.1, s32[3,1920]{1,0:T(4,128)} %lattice_hbm.1), custom_call_target="tpu_custom_call" | custom-call | tf_op jit(solution)/shard_map/exchange/pallas_call | solution.py:443
  43.0 3.3 %rotate.1 = bf16[1,8,13824]{2,1,0:T(8,128)(2,1)} custom-call(bf16[54,16,128]{2,1,0:T(8,128)(2,1)} %get-tuple-element.8.blk_hbm, bf16[128,256]{1,0:T(8,128)(2,1)} %get-tuple-element.9.lhs1_hbm, bf16[128,256]{1,0:T(8,128)(2,1)} %get-tuple-element.10.lhs2_hbm, s32[1,8]{1,0:T(1,128)} %counts_hbm.1), custom_call_target="tpu_custom_call" | custom-call | tf_op jit(solution)/shard_map/rotate/pallas_call | solution.py:482
